TPU v7x, 32 devices: a whole 2x2x4 slice. The times are simulated.
32 devices in a mesh: grp: 4 (over y, x), chan: 8 (over z, core).
Axes of the slice: x: 2, y: 2, z: 4, core: 2. Of those that a mesh axis runs over, the one named last changes fastest.
Arguments:
- voltages: bfloat16 [1024, 65536], P('grp', 'chan'), may hold values from -6 to 6
- prototype: float32 [8, 1024], replicated, may hold values from -2 to 2
Outputs:
- visibilities: bfloat16 [1024, 1024, 1024], P('chan', 'grp')
All inputs are finite; a program needn't handle non-finite values.
Results may differ from a plain program's by a relative error of at most 0.0072.
Values may be sent and summed in bfloat16 or wider, within the bound.
No kernel may reach another device: no remote copies, remote signals or barrier semaphores. Data moves between devices by JAX's collectives and lax.ppermute only.
A program may use at most 128 MiB of HBM per device.

v0:
```python
import math

import jax
import jax.numpy as jnp
from jax import lax
from jax.sharding import PartitionSpec as P


def shifted(block, axis, distance):
    devices = range(lax.axis_size(axis))
    route = [(i - distance, i) for i in devices if i - distance in devices]
    return lax.ppermute(block, axis, route)


def cosine_table(width):
    places = jnp.arange(width, dtype=jnp.int32)
    phase = (2 * places[:, None] + 1) * (2 * places[None, :] + 1) % (8 * width)
    return jnp.cos(phase.astype(jnp.float32) * (math.pi / (4 * width))).astype(jnp.bfloat16)


def fold_frames(extended, prototype, count):
    total = jnp.zeros((extended.shape[0], count, extended.shape[2]), jnp.float32)
    for tap_index in range(prototype.shape[0]):
        parity = 1.0 if tap_index % 2 == 0 else -1.0
        weights = parity * prototype[tap_index]
        total = total + weights[None, None, :] * extended[:, tap_index : tap_index + count].astype(
            jnp.float32
        )
    return total.astype(jnp.bfloat16)


def pair_products(left, right):
    summed = jnp.einsum("cti,ctj->cij", left, right, preferred_element_type=jnp.float32)
    return (summed / left.shape[1]).astype(jnp.bfloat16)


def on_device(voltages, prototype):
    depth = prototype.shape[0]
    width = prototype.shape[1]
    inputs_here = voltages.shape[0]
    frames_here = voltages.shape[1] // width
    framed = voltages.reshape(inputs_here, frames_here, width)
    following = shifted(framed[:, : depth - 1], "chan", -1)
    extended = jnp.concatenate([framed, following], axis=1)
    folded = fold_frames(extended, prototype, frames_here)
    table = cosine_table(width)
    product = jnp.einsum("itm,mk->kti", folded, table, preferred_element_type=jnp.float32)
    spectra = (product * math.sqrt(2.0 / width)).astype(jnp.bfloat16)
    turned = lax.all_to_all(spectra, "chan", split_axis=0, concat_axis=1, tiled=True)
    return pair_products(turned, lax.all_gather(turned, "grp", axis=2, tiled=True))


def solution(mesh):
    placed = (P("grp", "chan"), P())
    return jax.shard_map(
        on_device, mesh=mesh, in_specs=placed, out_specs=P("chan", "grp", None), check_vma=False
    )
```

profile of v0, /device:TPU:16, one launch (start us, length us, event | category | flops | bytes accessed | tf_op | source)
XLA Modules:
  0.0 392.1 jit_solution(2286057786033915777)
XLA Ops:
  6.5 0.0 all-gather.2.cloned.1.call-start
  6.5 0.0 copy-start.3
  6.5 0.0 copy-start.1
  6.5 2.8 copy.21
  9.3 0.5 slice.64
  9.9 1.9 collective-permute-start
  11.8 0.0 copy-done.3
  11.9 0.0 copy-done.1
  11.9 0.6 constant_dynamic-update-slice_fusion.1
  12.5 39.7 %collective-permute-done = bf16[256,7,1024]{2,0,1:T(8,128)(2,1)S(1)} collective-permute-done((bf16[256,7,1024]{2,0,1:T(8,128)(2,1)S(1)}, bf16[256,7,1024]{2,0,1:T(8,128)(2,1)S(1)}, u32[]{:S(2)}, u32[]{:S(2)}) %collective-permute-start) | collective-permute-done | bytes 3670048 | tf_op jit(solution)/shard_map/ppermute | solution.py:12
  52.2 0.5 constant_dynamic-update-slice_fusion
  52.8 0.0 copy-start.2
  52.8 3.2 copy-done.2
  56.0 33.1 %fusion.5 = bf16[1024,8,256]{2,0,1:T(8,128)(2,1)} fusion(bf16[256,15,1024]{2,0,1:T(8,128)(2,1)} %copy-done.2, f32[1024]{0:T(1024)S(1)} %bitcast.43, f32[1024]{0:T(1024)S(1)} %bitcast.44, f32[1024]{0:T(1024)S(1)} %bitcast.38, f32[1024]{0:T(1024)S(1)} %bitcast.39, f32[1024]{0:T(1024)S(1)} %bitcast.40, f32[1024]{0:T(1024)S(1)} %bitcast.41, ...), kind=kOutput, calls=%fused_computation.13 | convolution fusion | flops 4365221888 | bytes 37789696 | tf_op jit(solution)/shard_map/itm,mk->kti/dot_general | solution.py:47
  89.1 4.6 %copy.10 = bf16[1024,8,256]{2,1,0:T(8,128)(2,1)S(1)} copy(bf16[1024,8,256]{2,0,1:T(8,128)(2,1)} %fusion.5) | data formatting | bytes 8388608 | tf_op jit(solution)/shard_map/convert_element_type | solution.py:48
  93.7 96.2 %all_to_all.18 = bf16[1024,8,256]{2,1,0:T(8,128)(2,1)S(1)} all-to-all(bf16[1024,8,256]{2,1,0:T(8,128)(2,1)S(1)} %copy.10), channel_id=1, replica_groups=mesh['grp'=4,'chan'=8] {'chan'}, dimensions={0} | all-to-all | bytes 8388608 | tf_op jit(solution)/shard_map/all_to_all | solution.py:49
  189.8 0.0 copy-start
  189.8 1.9 copy-done
  191.8 2.6 copy.22
  194.4 0.0 all-gather.2.cloned.1.call-update
  194.4 159.1 %all-gather.2.cloned.1.call-done = bf16[128,64,1024]{2,1,0:T(8,128)(2,1)} async-done(((bf16[128,64,256]{2,1,0:T(8,128)(2,1)}), bf16[128,64,1024]{2,1,0:T(8,128)(2,1)}) %all-gather.2.cloned.1.call-update) | async-done | bytes 16777232 | tf_op jit(solution)/shard_map/all_gather | solution.py:50
  353.5 31.7 %multiply_convert_fusion = bf16[128,256,1024]{2,1,0:T(8,128)(2,1)} fusion(bf16[128,64,1024]{2,1,0:T(8,128)(2,1)} %all-gather.2.cloned.1.call-done, bf16[8,128,8,256]{3,2,1,0:T(8,128)(2,1)} %bitcast.31), kind=kOutput, calls=%fused_computation | convolution fusion | flops 4362076160 | bytes 88080384 | tf_op jit(solution)/shard_map/cti,ctj->cij/dot_general | solution.py:33
  (2 shorter events, 0.0 us)
Async XLA Ops:
  6.5 347.0 %all-gather.2.cloned.1.call-start = ((), (), s32[]{:S(2)}) async-start(), calls=%async_computation.1 | async-start | bytes 20971520 | tf_op jit(solution)/shard_map/all_gather | solution.py:50
  6.5 5.3 %copy-start.3 = (f32[8,1024]{1,0:T(8,128)S(1)}, f32[8,1024]{1,0:T(8,128)}, u32[]{:S(2)}) copy-start(f32[8,1024]{1,0:T(8,128)} %param.3) | copy-start | bytes 98308
  6.5 5.3 %copy-start.1 = (bf16[256,8192]{1,0:T(8,128)(2,1)S(1)}, bf16[256,8192]{1,0:T(8,128)(2,1)}, u32[]{:S(2)}) copy-start(bf16[256,8192]{1,0:T(8,128)(2,1)} %param.2) | copy-start | bytes 12582916
  9.9 42.3 %collective-permute-start = (bf16[256,7,1024]{2,0,1:T(8,128)(2,1)S(1)}, bf16[256,7,1024]{2,0,1:T(8,128)(2,1)S(1)}, u32[]{:S(2)}, u32[]{:S(2)}) collective-permute-start(bf16[256,7,1024]{2,0,1:T(8,128)(2,1)S(1)} %slice.64), channel_id=1, source_target_pairs={{1,0},{2,1},{3,2},{4,3},{5,4},{6,5},{7,6},{9,8},{10,9},{11,10},{12... | collective-permute-start | bytes 11010056 | tf_op jit(solution)/shard_map/ppermute | solution.py:12
  52.8 3.2 copy-start.2
  189.8 1.9 copy-start
Sparse Core Ops, SparseCore 0:
  194.5 158.9 all-gather.1
where the time goes:
time: 394 us; the launch traced here: 392 us
  waiting for transfers between devices  199 us (51%)
  blocking collectives  96.2 us (24%)
  matrix products  64.9 us (16%)
  local copies, waits for them, and re-layouts  16.8 us (4%)
  between operations  13.5 us (3%)
    all_gather x1, waiting for transfers between devices, on_device(): lax.all_gather(turned, 'grp', axis=2, tiled=True)  159 us
    all_to_all x1, blocking collectives, on_device(): lax.all_to_all(spectra, 'chan', split_axis=0, concat_axis=1, tiled=True)  96.2 us
    ppermute x1, waiting for transfers between devices, shifted(): return lax.ppermute(block, axis, route)  39.7 us
    dot_general x1, matrix products, on_device(): jnp.einsum('itm,mk->kti', folded, table, preferred_element_type=jnp.float32)  33.1 us
    dot_general x1, matrix products, pair_products(): jnp.einsum('cti,ctj->cij', left, right, preferred_element_type=jnp.float32)  31.7 us
  transfers between devices with their start and end apart: 2, of which 2 were waited for; matrix products, arithmetic and copies ran while one was open for 0% of the time, Pallas kernels for 0%

commit v1 on v0

v1 whole, which is shorter than its diff:
```python
import functools
import math

import jax
import jax.numpy as jnp
from jax import lax
from jax.experimental import pallas as pl
from jax.experimental.pallas import tpu as pltpu
from jax.sharding import PartitionSpec as P

BOUNDS = (0, 11, 16)
CALLS = ((0, 6, 11), (11, 16))
ROW_STEPS = 4
PAIRS = 2
FOLD_VMEM = 28 * 1024 * 1024
CORRELATE_VMEM = 60 * 1024 * 1024


def swap(block, axis, bit):
    return lax.ppermute(block, axis, [(i, i ^ bit) for i in range(lax.axis_size(axis))])


def after(value, *events):
    return lax.optimization_barrier((value,) + events)[0]


def cosine_rows(starts, count, width):
    fine = math.gcd(count, 32)
    places = 2 * jnp.arange(width, dtype=jnp.int32)[None, :] + 1
    turns = lambda steps: (steps[:, None] * places % (8 * width)).astype(jnp.float32) * (
        math.pi / (4 * width)
    )
    blocks = starts[:, None] + fine * jnp.arange(count // fine, dtype=jnp.int32)[None, :]
    coarse_turn = turns(2 * blocks.reshape(-1))
    fine_turn = turns(2 * jnp.arange(fine, dtype=jnp.int32) + 1)
    trig = [jnp.cos(coarse_turn), jnp.sin(coarse_turn), jnp.cos(fine_turn), jnp.sin(fine_turn)]
    cos_a, sin_a, cos_b, sin_b = lax.optimization_barrier(trig)
    table = cos_a[:, None] * cos_b[None] - sin_a[:, None] * sin_b[None]
    return table.reshape(-1, width).astype(jnp.bfloat16)


def spectra_kernel(late, cuts, scale, core_ref, weights_ref, table_ref, *refs):
    sources = 4 if late else 2
    inputs, outs = refs[:sources], refs[sources:-4]
    samples, folded, spread, sems = refs[-4:]
    core = core_ref[0]
    own, other = inputs[0], inputs[1]
    count, width = folded.shape[1], folded.shape[2]
    depth, frames = weights_ref.shape[0], folded.shape[0]
    slab, tail = frames * width, (depth - 1) * width
    step_rows = count // ROW_STEPS
    half_rows = count // 2

    def slab_copy(ref, step, columns, start, which):
        rows = pl.ds(step * step_rows, step_rows)
        return pltpu.make_async_copy(
            ref.at[rows, pl.ds(0, columns)],
            samples.at[rows, pl.ds(start, columns)],
            sems.at[which, step],
        )

    def halo_copy(ref, step):
        rows = pl.ds(step * step_rows, step_rows)
        return pltpu.make_async_copy(
            ref.at[pl.ds(step * step_rows % half_rows, step_rows), :],
            samples.at[rows, pl.ds(slab, tail)],
            sems.at[1, step],
        )

    def start_all(first, second):
        for step in range(ROW_STEPS):
            slab_copy(first, step, slab, 0, 0).start()
            if not late:
                slab_copy(second, step, tail, slab, 1).start()

    head_core = 1 if late else 0

    @pl.when(core == head_core)
    def _():
        start_all(own, other)

    @pl.when(core != head_core)
    def _():
        start_all(other, own)

    if late:
        for step in range(ROW_STEPS):
            half = step * step_rows // half_rows

            @pl.when(core == half)
            def _():
                halo_copy(inputs[2], step).start()

            @pl.when(core != half)
            def _():
                halo_copy(inputs[3], step).start()

    for step in range(ROW_STEPS):
        slab_copy(own, step, slab, 0, 0).wait()
        if late:
            halo_copy(inputs[2], step).wait()
        else:
            slab_copy(own, step, tail, slab, 1).wait()

        def fold(tile, carry):
            lanes = pl.multiple_of(tile * 128, 128)
            taps = [
                jnp.broadcast_to(weights_ref[pl.ds(tap, 1), pl.ds(lanes, 128)], (16, 128))
                for tap in range(depth)
            ]
            for block in range(step_rows // 16):
                rows = pl.ds(step * step_rows + block * 16, 16)
                window = [
                    samples[rows, pl.ds(pl.multiple_of(lanes + place * width, 128), 128)].astype(
                        jnp.float32
                    )
                    for place in range(frames + depth - 1)
                ]
                for frame in range(frames):
                    total = taps[0] * window[frame]
                    for tap in range(1, depth):
                        total = total + taps[tap] * window[frame + tap]
                    folded[frame, rows, pl.ds(lanes, 128)] = total.astype(jnp.bfloat16)
            return carry

        lax.fori_loop(0, width // 128, fold, 0)

    channels = table_ref.shape[0]
    for frame in range(frames):
        product = scale * lax.dot_general(
            table_ref[...],
            folded[frame],
            (((1,), (1,)), ((), ())),
            preferred_element_type=jnp.float32,
        )
        for half in range(count // 128):
            spread[half, pl.ds(frame, channels, stride=frames), :] = product[
                :, half * 128 : half * 128 + 128
            ]
    for (first, rows), out in zip(cuts, outs):
        for half in range(count // 128):
            out[:, half * 128 : half * 128 + 128] = spread[half, first : first + rows, :].astype(
                jnp.bfloat16
            )


def spectra_blocks(late, cuts, core, weights, table, sources):
    count = sources[0].shape[0]
    depth, width = weights.shape
    frames = sources[0].shape[1] // width
    channels = table.shape[0]
    cuts = [(first * frames, rows * frames) for first, rows in cuts]
    whole = pl.BlockSpec(memory_space=pltpu.VMEM)
    return pl.pallas_call(
        functools.partial(spectra_kernel, late, cuts, math.sqrt(2.0 / width)),
        out_shape=[jax.ShapeDtypeStruct((rows, count), jnp.bfloat16) for _, rows in cuts],
        in_specs=[pl.BlockSpec(memory_space=pltpu.SMEM), whole, whole]
        + [pl.BlockSpec(memory_space=pl.ANY)] * len(sources),
        out_specs=[whole] * len(cuts),
        scratch_shapes=[
            pltpu.VMEM((count, (frames + depth - 1) * width), jnp.bfloat16),
            pltpu.VMEM((frames, count, width), jnp.bfloat16),
            pltpu.VMEM((count // 128, channels * frames, 128), jnp.float32),
            pltpu.SemaphoreType.DMA((2, ROW_STEPS)),
        ],
        compiler_params=pltpu.CompilerParams(vmem_limit_bytes=FOLD_VMEM),
        cost_estimate=pl.CostEstimate(flops=1, bytes_accessed=1, transcendentals=0),
        name="fold_transform",
    )(core, weights, table, *sources)


def correlate_kernel(scale, groups, ordered, first, group_ref, *refs):
    out, held, sems = refs[-3:]
    count = out.shape[1]
    group = group_ref[0]
    step, steps = pl.program_id(0), pl.num_programs(0)
    slot = step % 2
    pieces, used = [], 0
    for is_ordered in ordered:
        members = refs[used : used + (1 if is_ordered else groups)]
        used += len(members)
        pieces += [(is_ordered, members, part) for part in range(members[0].shape[-3])]

    def copy(where, channel):
        target = first + step * 2 * PAIRS + channel
        return pltpu.make_async_copy(held.at[where, channel], out.at[target], sems.at[where, channel])

    def wait_all(where):
        for channel in range(2 * PAIRS):
            copy(where, channel).wait()

    @pl.when(step >= 2)
    def _():
        wait_all(slot)

    depth = len(pieces) * 16
    places = lax.broadcasted_iota(jnp.int32, (count, depth), 1)
    even = jnp.where(places % 16 < 8, scale, 0.0).astype(jnp.bfloat16)
    odd = jnp.where(places % 16 < 8, 0.0, scale).astype(jnp.bfloat16)
    for pair in range(PAIRS):
        rows = slice(pair * 16, pair * 16 + 16)

        def stack(member):
            return jnp.concatenate(
                [
                    members[0][group ^ member, part, rows, :]
                    if is_ordered
                    else members[member][part, rows, :]
                    for is_ordered, members, part in pieces
                ],
                axis=0,
            )

        turned = stack(0).T
        left = jnp.concatenate([turned * even, turned * odd], axis=0)
        for member in range(groups):
            summed = lax.dot_general(
                left, stack(member), (((1,), (0,)), ((), ())), preferred_element_type=jnp.float32
            )
            columns = pl.ds(pl.multiple_of((group ^ member) * count, 128), count)
            result = summed.astype(jnp.bfloat16)
            held[slot, 2 * pair, :, columns] = result[:count]
            held[slot, 2 * pair + 1, :, columns] = result[count:]
        copy(slot, 2 * pair).start()
        copy(slot, 2 * pair + 1).start()

    @pl.when(step == steps - 1)
    def _():
        wait_all(slot)

    @pl.when((step == steps - 1) & (steps > 1))
    def _():
        wait_all(1 - slot)


def correlate(frames, first, stop, start, channels, group, wide, narrow, earlier):
    groups, count = lax.axis_size("grp"), (wide + narrow)[0][-1].shape[-1]
    block = 2 * PAIRS
    base, steps = first // block, (stop - first) // block
    pieces = [(piece, base) for piece in wide] + [
        (piece, (first - start) // block) for piece in narrow
    ]
    ordered = [len(piece) == 1 for piece, _ in pieces]
    operands = [array for piece, _ in pieces for array in piece]
    aliases = {} if earlier is None else {1 + len(operands): 0}
    carried = [] if earlier is None else [earlier]

    def spec(array, start):
        if len(array.shape) == 4:
            return pl.BlockSpec(
                (groups, array.shape[1], 16 * PAIRS, count), lambda i, ref: (0, 0, start + i, 0)
            )
        return pl.BlockSpec((array.shape[0], 16 * PAIRS, count), lambda i, ref: (0, start + i, 0))

    return pl.pallas_call(
        functools.partial(correlate_kernel, 1.0 / frames, groups, ordered, first),
        out_shape=jax.ShapeDtypeStruct((channels, count, groups * count), jnp.bfloat16),
        grid_spec=pltpu.PrefetchScalarGridSpec(
            num_scalar_prefetch=1,
            grid=(steps,),
            in_specs=[spec(array, start) for piece, start in pieces for array in piece]
            + [pl.BlockSpec(memory_space=pl.ANY)] * len(carried),
            out_specs=pl.BlockSpec(memory_space=pl.ANY),
            scratch_shapes=[
                pltpu.VMEM((2, block, count, groups * count), jnp.bfloat16),
                pltpu.SemaphoreType.DMA((2, block)),
            ],
        ),
        input_output_aliases=aliases,
        compiler_params=pltpu.CompilerParams(vmem_limit_bytes=CORRELATE_VMEM),
        cost_estimate=pl.CostEstimate(flops=1, bytes_accessed=1, transcendentals=0),
        name="correlate",
    )(group, *operands, *carried)


def joined(block, turn, earlier=(), events=()):
    groups = lax.axis_size("grp")
    bits = [1 << b for b in range(groups.bit_length() - 1)]
    bits = bits[turn % len(bits) :] + bits[: turn % len(bits)]
    held = {bit: swap(after(block, *earlier), "grp", bit) for bit in bits}
    direct = tuple(held[bit] for bit in bits)
    reached = bits[:1]
    for bit in bits[1:]:
        for member in list(reached):
            held[member | bit] = swap(after(held[member], *direct, *events), "grp", bit)
        reached += [bit] + [member | bit for member in reached]
    held[0] = block
    return [held[member] for member in range(groups)], direct


def on_device(voltages, prototype):
    depth, width = prototype.shape
    owners = lax.axis_size("chan")
    parts = owners // 2
    channels = width // owners
    frames_here = voltages.shape[1] // width
    frames = frames_here * owners
    place = lax.axis_index("chan")
    core = place % 2
    group = lax.axis_index("grp")
    half = voltages.shape[0] // 2

    other = swap(voltages, "chan", 1)
    route = [[(2 * p + 2, 2 * p + k) for p in range(parts - 1)] for k in (0, 1)]
    tail = (depth - 1) * width
    sliced = [voltages[k * half : k * half + half, :tail] for k in (0, 1)]
    ahead = [lax.ppermute(sliced[k], "chan", route[k]) for k in (0, 1)]
    other = after(other, *sliced)

    owned = (place // 2) ^ jnp.arange(parts, dtype=jnp.int32)
    table = cosine_rows((owned * 2 + core) * channels, channels, width)
    signs = jnp.where(jnp.arange(depth) % 2 == 0, 1.0, -1.0).astype(jnp.float32)
    weights = signs[:, None] * prototype
    at_core = core.reshape(1)

    bounds = [round(channels * bound / 64) * 4 for bound in BOUNDS]
    blocks = list(zip(bounds[:-1], bounds[1:]))
    cuts = [(0, channels), (channels, channels)] + [
        (part * channels + first, stop - first) for first, stop in blocks for part in range(2, parts)
    ]
    early = spectra_blocks(False, cuts, at_core, weights, table, [voltages, other])
    own_early, sent = joined(early[0][None], 0)
    ahead = lax.optimization_barrier((ahead[0], ahead[1], *own_early[1:]))
    halo = jnp.where(core == 0, ahead[0], ahead[1])
    other_halo = swap(halo, "chan", 1)

    near = swap(after(early[1], ahead[0], ahead[1]), "chan", 2)
    early_parts = [early[2 + i * (parts - 2) :][: parts - 2] for i in range(len(blocks))]
    middle = swap(after(early_parts[0][0], ahead[0], ahead[1]), "chan", 4)
    near, middle = lax.optimization_barrier((near, middle))
    near_joined, sent = joined(near[None], 1, sent)

    cuts = [(first, stop - first) for first, stop in blocks] + [
        (part * channels + first, stop - first) for first, stop in blocks for part in range(1, parts)
    ]
    late = spectra_blocks(
        True, cuts, at_core, weights, table, [voltages, other, halo, after(other_halo, near)]
    )
    moved, landed = [], ()
    for index in range(len(blocks)):
        if index > 0:
            middle = swap(after(early_parts[index][0], *landed), "chan", 4)
        waits = (middle,) if index == 0 else landed
        far = [
            swap(after(early_parts[index][part - 2], *waits), "chan", 2 * part)
            for part in range(3, parts)
        ]
        late_parts = late[len(blocks) + index * (parts - 1) :][: parts - 1]
        hops = [
            swap(after(late_parts[part - 1], middle, *far), "chan", 2 * part)
            for part in range(1, parts)
        ]
        landed = tuple(hops)
        moved.append((jnp.stack([late[index], middle] + far), jnp.stack(hops)))

    wide, results = [own_early, near_joined], [None]
    for index, (first, stop) in enumerate(blocks):
        ready, own_sent = joined(moved[index][0], 0, sent, results[1:2])
        if index == 0:
            sent = own_sent + tuple(near_joined[1:])
        rest, own_sent = joined(
            moved[index][1], 1, sent, results[1:2] if index > 0 else landed
        )
        sent = own_sent
        calls = [round(channels * bound / 64) * 4 for bound in CALLS[index]]
        for call_first, call_stop in zip(calls[:-1], calls[1:]):
            results.append(
                correlate(
                    frames,
                    call_first,
                    call_stop,
                    first,
                    channels,
                    group.reshape(1),
                    wide,
                    [ready, rest],
                    results[-1],
                )
            )
    return results[-1]


def solution(mesh):
    placed = (P("grp", "chan"), P())
    return jax.shard_map(
        on_device, mesh=mesh, in_specs=placed, out_specs=P("chan", "grp", None), check_vma=False
    )
```

time: 394 us -> 240 us (0.61)
  blocking collectives: 96.2 us -> 0 us
  waiting for transfers between devices: 199 us -> 121 us
  matrix products: 64.9 us -> 0 us
  Pallas kernels: 0 us -> 62.8 us
  starting transfers between devices: 1.92 us -> 38.9 us
  between operations: 13.5 us -> 0.55 us
  local copies, waits for them, and re-layouts: 16.8 us -> 9.97 us
    all_gather x1 -> x0, waiting for transfers between devices: 159 us -> none  [on_device(): lax.all_gather(turned, 'grp', axis=2, tiled=True)]
    all_to_all x1 -> x0, blocking collectives: 96.2 us -> none  [on_device(): lax.all_to_all(spectra, 'chan', split_axis=0, concat_axis=1, tiled=True)]
    ppermute x1 -> x33, waiting for transfers between devices: 39.7 us -> 121 us  [the longest x31 112 us: swap(): lax.ppermute(block, axis, [(i, i ^ bit) for i in range(lax.axis_size(axis...]
    dot_general x2 -> x0, matrix products: 64.9 us -> none  [the longest x1 33.1 us: on_device(): jnp.einsum('itm,mk->kti', folded, table, preferred_element_type=jnp.float32)]
    pallas_call x0 -> x5, Pallas kernels: none -> 62.8 us  [the longest x3 44.1 us: correlate(): pl.pallas_call(functools.partial(correlate_kernel, 1.0 / frames, groups,...]
    ppermute x1 -> x33, starting transfers between devices: 1.92 us -> 38.9 us  [the longest x31 33.2 us: swap(): lax.ppermute(block, axis, [(i, i ^ bit) for i in range(lax.axis_size(axis...]
    convert_element_type x1 -> x0, local copies, waits for them, and re-layouts: 4.56 us -> none  [on_device(): spectra = (product * math.sqrt(2.0 / width)).astype(jnp.bfloat16)]
  transfers between devices with their start and end apart: 2 -> 33, of which waited for: 2 -> 17; matrix products, arithmetic and copies ran while one was open for 0% -> 3% of each run, Pallas kernels for 0% -> 21%
where the time goes in v1:
time: 240 us; the launch traced here: 236 us
  waiting for transfers between devices  121 us (50%)
  Pallas kernels  62.8 us (26%)
  starting transfers between devices  38.9 us (16%)
  local copies, waits for them, and re-layouts  9.97 us (4%)
  other arithmetic  3.44 us (1%)
    ppermute x31, waiting for transfers between devices, swap(): lax.ppermute(block, axis, [(i, i ^ bit) for i in range(lax.axis_size(axis...  112 us
    pallas_call x3, Pallas kernels, correlate(): pl.pallas_call(functools.partial(correlate_kernel, 1.0 / frames, groups,...  44.1 us
    ppermute x31, starting transfers between devices, swap(): lax.ppermute(block, axis, [(i, i ^ bit) for i in range(lax.axis_size(axis...  33.2 us
    pallas_call x2, Pallas kernels, spectra_blocks(): pl.pallas_call(functools.partial(spectra_kernel, late, cuts, math.sqrt(2....  18.7 us
    ppermute x2, waiting for transfers between devices, on_device(): ahead = [lax.ppermute(sliced[k], 'chan', route[k]) for k in (0, 1)]  8.76 us
    ppermute x2, starting transfers between devices, on_device(): ahead = [lax.ppermute(sliced[k], 'chan', route[k]) for k in (0, 1)]  5.7 us
    unnamed x42, local copies, waits for them, and re-layouts  5.67 us
  transfers between devices with their start and end apart: 33, of which 17 were waited for; matrix products, arithmetic and copies ran while one was open for 3% of the time, Pallas kernels for 21%

profile of v1, /device:TPU:16, one launch (start us, length us, event | category | flops | bytes accessed | tf_op | source)
XLA Modules:
  0.0 236.4 jit_solution(1053669794893117596)
XLA Ops:
  0.0 4.2 %fusion.10 = (bf16[128,7168]{1,0:T(8,128)(2,1)}, bf16[128,7168]{1,0:T(8,128)(2,1)}) fusion(bf16[256,8192]{1,0:T(8,128)(2,1)} %refs_0_.3), kind=kLoop, calls=%fused_computation.34 | loop fusion | bytes 7340032 | tf_op jit(solution)/shard_map/slice | solution.py:306
  4.2 2.3 collective-permute-start.4
  6.6 3.4 %collective-permute-start.5 = (bf16[128,7168]{1,0:T(8,128)(2,1)}, bf16[128,7168]{1,0:T(8,128)(2,1)}, u32[]{:S(2)}, u32[]{:S(2)}) collective-permute-start(bf16[128,7168]{1,0:T(8,128)(2,1)} %get-tuple-element.97), channel_id=1, source_target_pairs={{2,1},{4,3},{6,5},{10,9},{12,11},{14,13},{18,17},{20,19},{22,21},{... | collective-permute-start | bytes 5505032 | tf_op jit(solution)/shard_map/ppermute | solution.py:307
  11.5 2.2 copy-done
  13.6 9.4 %fold_transform.2 = (bf16[1024,256]{1,0:T(8,128)(2,1)S(1)}, bf16[1024,256]{1,0:T(8,128)(2,1)S(1)}, bf16[704,256]{1,0:T(8,128)(2,1)S(1)}, bf16[704,256]{1,0:T(8,1...) custom-call(s32[1]{0:T(128)} %bitcast.1.core_ref, ...), custom_call_target="tpu_custom_call" | custom-call | flops 1 | bytes 1 | tf_op jit(solution)/shard_map/fold_transform/pallas_call | solution.py:154
  26.1 9.0 %collective-permute-done.1.refs_1_ = bf16[1,1024,256]{2,1,0:T(8,128)(2,1)} collective-permute-done((bf16[1,1024,256]{2,1,0:T(8,128)(2,1)S(1)}, bf16[1,1024,256]{2,1,0:T(8,128)(2,1)}, u32[]{:S(2)}, u32[]{:S(2)}) %collective-permute-start.1) | collective-permute-done | bytes 524320 | tf_op jit(solution)/shard_map/ppermute | solution.py:20
  38.5 8.8 %collective-permute-done.5 = bf16[128,7168]{1,0:T(8,128)(2,1)} collective-permute-done((bf16[128,7168]{1,0:T(8,128)(2,1)}, bf16[128,7168]{1,0:T(8,128)(2,1)}, u32[]{:S(2)}, u32[]{:S(2)}) %collective-permute-start.5) | collective-permute-done | bytes 1835040 | tf_op jit(solution)/shard_map/ppermute | solution.py:307
  48.1 1.7 broadcast_select_fusion.refs_2_
  52.8 20.2 %collective-permute-done.7 = bf16[704,256]{1,0:T(8,128)(2,1)S(1)} collective-permute-done((bf16[704,256]{1,0:T(8,128)(2,1)S(1)}, bf16[704,256]{1,0:T(8,128)(2,1)S(1)}, u32[]{:S(2)}, u32[]{:S(2)}) %collective-permute-start.7) | collective-permute-done | bytes 360480 | tf_op jit(solution)/shard_map/ppermute | solution.py:20
  75.4 1.6 collective-permute-start.12
  77.0 9.3 %fold_transform.3 = (bf16[704,256]{1,0:T(8,128)(2,1)S(1)}, bf16[320,256]{1,0:T(8,128)(2,1)S(1)}, bf16[704,256]{1,0:T(8,128)(2,1)S(1)}, bf16[704,256]{1,0:T(8,128...) custom-call(s32[1]{0:T(128)} %bitcast.1.core_ref, ...), custom_call_target="tpu_custom_call" | custom-call | flops 1 | bytes 1 | tf_op jit(solution)/shard_map/fold_transform/pallas_call | solution.py:154
  86.4 17.5 %collective-permute-done.12 = bf16[704,256]{1,0:T(8,128)(2,1)S(1)} collective-permute-done((bf16[704,256]{1,0:T(8,128)(2,1)S(1)}, bf16[704,256]{1,0:T(8,128)(2,1)S(1)}, u32[]{:S(2)}, u32[]{:S(2)}) %collective-permute-start.12) | collective-permute-done | bytes 360480 | tf_op jit(solution)/shard_map/ppermute | solution.py:20
  104.1 2.7 %collective-permute-start.18 = (bf16[3,704,256]{2,1,0:T(8,128)(2,1)S(1)}, bf16[3,704,256]{2,1,0:T(8,128)(2,1)S(1)}, u32[]{:S(2)}, u32[]{:S(2)}) collective-permute-start(bf16[3,704,256]{2,1,0:T(8,128)(2,1)S(1)} %pad_maximum_fusion.1.refs_8_), channel_id=1, source_target_pairs={{0,8},{8,0},{16,24},{24,16},{1,9},{9,1},{17,25},{25,17},{2,10},{10... | collective-permute-start | bytes 3244040 | tf_op jit(solution)/shard_map/ppermute | solution.py:20
  108.8 10.5 %collective-permute-done.15 = bf16[704,256]{1,0:T(8,128)(2,1)S(1)} collective-permute-done((bf16[704,256]{1,0:T(8,128)(2,1)S(1)}, bf16[704,256]{1,0:T(8,128)(2,1)S(1)}, u32[]{:S(2)}, u32[]{:S(2)}) %collective-permute-start.15) | collective-permute-done | bytes 360480 | tf_op jit(solution)/shard_map/ppermute | solution.py:20
  119.2 2.9 %collective-permute-done.14 = bf16[704,256]{1,0:T(8,128)(2,1)S(1)} collective-permute-done((bf16[704,256]{1,0:T(8,128)(2,1)S(1)}, bf16[704,256]{1,0:T(8,128)(2,1)S(1)}, u32[]{:S(2)}, u32[]{:S(2)}) %collective-permute-start.14) | collective-permute-done | bytes 360480 | tf_op jit(solution)/shard_map/ppermute | solution.py:20
  122.2 6.7 %collective-permute-done.13 = bf16[704,256]{1,0:T(8,128)(2,1)S(1)} collective-permute-done((bf16[704,256]{1,0:T(8,128)(2,1)S(1)}, bf16[704,256]{1,0:T(8,128)(2,1)S(1)}, u32[]{:S(2)}, u32[]{:S(2)}) %collective-permute-start.13) | collective-permute-done | bytes 360480 | tf_op jit(solution)/shard_map/ppermute | solution.py:20
  129.0 8.1 %collective-permute-done.10.refs_7_ = bf16[1,1024,256]{2,1,0:T(8,128)(2,1)S(1)} collective-permute-done((bf16[1,1024,256]{2,1,0:T(8,128)(2,1)S(1)}, bf16[1,1024,256]{2,1,0:T(8,128)(2,1)S(1)}, u32[]{:S(2)}, u32[]{:S(2)}) %collective-permute-start.10) | collective-permute-done | bytes 524320 | tf_op jit(solution)/shard_map/ppermute | solution.py:20
  137.2 2.2 collective-permute-start.21
  139.4 1.9 collective-permute-start.24
  141.4 5.3 %collective-permute-done.16 = bf16[320,256]{1,0:T(8,128)(2,1)S(1)} collective-permute-done((bf16[320,256]{1,0:T(8,128)(2,1)S(1)}, bf16[320,256]{1,0:T(8,128)(2,1)S(1)}, u32[]{:S(2)}, u32[]{:S(2)}) %collective-permute-start.16) | collective-permute-done | bytes 163872 | tf_op jit(solution)/shard_map/ppermute | solution.py:20
  146.7 2.4 %collective-permute-done.17 = bf16[320,256]{1,0:T(8,128)(2,1)S(1)} collective-permute-done((bf16[320,256]{1,0:T(8,128)(2,1)S(1)}, bf16[320,256]{1,0:T(8,128)(2,1)S(1)}, u32[]{:S(2)}, u32[]{:S(2)}) %collective-permute-start.17) | collective-permute-done | bytes 163872 | tf_op jit(solution)/shard_map/ppermute | solution.py:20
  150.0 2.2 collective-permute-start.26
  152.3 5.6 %collective-permute-done.27 = bf16[320,256]{1,0:T(8,128)(2,1)S(1)} collective-permute-done((bf16[320,256]{1,0:T(8,128)(2,1)S(1)}, bf16[320,256]{1,0:T(8,128)(2,1)S(1)}, u32[]{:S(2)}, u32[]{:S(2)}) %collective-permute-start.27) | collective-permute-done | bytes 163872 | tf_op jit(solution)/shard_map/ppermute | solution.py:20
  158.1 5.0 %collective-permute-done.25 = bf16[320,256]{1,0:T(8,128)(2,1)S(1)} collective-permute-done((bf16[320,256]{1,0:T(8,128)(2,1)S(1)}, bf16[320,256]{1,0:T(8,128)(2,1)S(1)}, u32[]{:S(2)}, u32[]{:S(2)}) %collective-permute-start.25) | collective-permute-done | bytes 163872 | tf_op jit(solution)/shard_map/ppermute | solution.py:20
  166.7 1.6 collective-permute-start.22
  168.4 10.5 %collective-permute-done.24.refs_11_ = bf16[3,704,256]{2,1,0:T(8,128)(2,1)S(1)} collective-permute-done((bf16[3,704,256]{2,1,0:T(8,128)(2,1)S(1)}, bf16[3,704,256]{2,1,0:T(8,128)(2,1)S(1)}, u32[]{:S(2)}, u32[]{:S(2)}) %collective-permute-start.24) | collective-permute-done | bytes 1081376 | tf_op jit(solution)/shard_map/ppermute | solution.py:20
  180.4 6.0 %collective-permute-done.28.refs_15_ = bf16[3,704,256]{2,1,0:T(8,128)(2,1)} collective-permute-done((bf16[3,704,256]{2,1,0:T(8,128)(2,1)}, bf16[3,704,256]{2,1,0:T(8,128)(2,1)}, u32[]{:S(2)}, u32[]{:S(2)}) %collective-permute-start.28) | collective-permute-done | bytes 1081376 | tf_op jit(solution)/shard_map/ppermute | solution.py:20
  186.4 16.3 %correlate.3.refs_16_ = bf16[128,256,1024]{2,1,0:T(8,128)(2,1)} custom-call(s32[1]{0:T(128)} %bitcast.group_ref, bf16[1,1024,256]{2,1,0:T(8,128)(2,1)} %bitcast.21, bf16[1,1024,256]{2,1,0:T(8,128)(2,1)} %collective-permute-done.1.refs_1_, bf16[1,1024,256]{2,1,0:T(8,128)(2,1)} %copy-done.5, bf16[1,1024,256]{2,1,0:T(8,128)(2,1)} %collective-permute-done.3.refs_3_, ...), custom_call_target="tpu_custom_call" | custom-call | flops 1 | bytes 1 | tf_op jit(solution)/shard_map/correlate/pallas_call | solution.py:255
  202.8 2.2 collective-permute-start.32
  205.0 1.8 collective-permute-start.29
  206.8 13.9 %correlate.4.refs_16_ = bf16[128,256,1024]{2,1,0:T(8,128)(2,1)} custom-call(s32[1]{0:T(128)} %bitcast.group_ref, bf16[1,1024,256]{2,1,0:T(8,128)(2,1)} %bitcast.22, bf16[1,1024,256]{2,1,0:T(8,128)(2,1)} %collective-permute-done.1.refs_1_, bf16[1,1024,256]{2,1,0:T(8,128)(2,1)} %copy-done.5, ...), custom_call_target="tpu_custom_call", output_to_operand_aliasing={{}: (17, {})} | custom-call | flops 1 | bytes 1 | tf_op jit(solution)/shard_map/correlate/pallas_call | solution.py:255
  222.3 13.9 %correlate.5 = bf16[128,256,1024]{2,1,0:T(8,128)(2,1)} custom-call(s32[1]{0:T(128)} %bitcast.group_ref, bf16[1,1024,256]{2,1,0:T(8,128)(2,1)} %bitcast.23, bf16[1,1024,256]{2,1,0:T(8,128)(2,1)} %collective-permute-done.1.refs_1_, bf16[1,1024,256]{2,1,0:T(8,128)(2,1)} %copy-done.5, ...), custom_call_target="tpu_custom_call", output_to_operand_aliasing={{}: (17, {})} | custom-call | flops 1 | bytes 1 | tf_op jit(solution)/shard_map/correlate/pallas_call | solution.py:255
  (97 shorter events, 24.5 us)
Async XLA Ops:
  0.0 11.4 %collective-permute-start = (bf16[256,8192]{1,0:T(8,128)(2,1)}, bf16[256,8192]{1,0:T(8,128)(2,1)}, u32[]{:S(2)}, u32[]{:S(2)}) collective-permute-start(bf16[256,8192]{1,0:T(8,128)(2,1)} %refs_0_.3), channel_id=1, source_target_pairs={{0,1},{1,0},{2,3},{3,2},{4,5},{5,4},{6,7},{7,6},{8,9},{9,8},{10,11... | collective-permute-start | bytes 12582920 | tf_op jit(solution)/shard_map/ppermute | solution.py:20
  4.2 34.3 %collective-permute-start.4 = (bf16[128,7168]{1,0:T(8,128)(2,1)}, bf16[128,7168]{1,0:T(8,128)(2,1)}, u32[]{:S(2)}, u32[]{:S(2)}) collective-permute-start(bf16[128,7168]{1,0:T(8,128)(2,1)} %get-tuple-element.98), channel_id=1, source_target_pairs={{2,0},{4,2},{6,4},{10,8},{12,10},{14,12},{18,16},{20,18},{22,20},{... | collective-permute-start | bytes 5505032 | tf_op jit(solution)/shard_map/ppermute | solution.py:307
  6.6 40.7 %collective-permute-start.5 = (bf16[128,7168]{1,0:T(8,128)(2,1)}, bf16[128,7168]{1,0:T(8,128)(2,1)}, u32[]{:S(2)}, u32[]{:S(2)}) collective-permute-start(bf16[128,7168]{1,0:T(8,128)(2,1)} %get-tuple-element.97), channel_id=1, source_target_pairs={{2,1},{4,3},{6,5},{10,9},{12,11},{14,13},{18,17},{20,19},{22,21},{... | collective-permute-start | bytes 5505032 | tf_op jit(solution)/shard_map/ppermute | solution.py:307
  23.0 12.0 %collective-permute-start.1 = (bf16[1,1024,256]{2,1,0:T(8,128)(2,1)S(1)}, bf16[1,1024,256]{2,1,0:T(8,128)(2,1)}, u32[]{:S(2)}, u32[]{:S(2)}) collective-permute-start(bf16[1,1024,256]{2,1,0:T(8,128)(2,1)S(1)} %bitcast.19), channel_id=1, source_target_pairs={{0,8},{8,0},{16,24},{24,16},{1,9},{9,1},{17,25},{25,17},{2,10},{10... | collective-permute-start | bytes 1572872 | tf_op jit(solution)/shard_map/ppermute | solution.py:20
  24.6 11.6 %collective-permute-start.2 = (bf16[1,1024,256]{2,1,0:T(8,128)(2,1)S(1)}, bf16[1,1024,256]{2,1,0:T(8,128)(2,1)S(1)}, u32[]{:S(2)}, u32[]{:S(2)}) collective-permute-start(bf16[1,1024,256]{2,1,0:T(8,128)(2,1)S(1)} %bitcast.20), channel_id=1, source_target_pairs={{0,16},{8,24},{16,0},{24,8},{1,17},{9,25},{17,1},{25,9},{2,18},{10... | collective-permute-start | bytes 1572872 | tf_op jit(solution)/shard_map/ppermute | solution.py:20
  37.0 11.1 %collective-permute-start.3 = (bf16[1,1024,256]{2,1,0:T(8,128)(2,1)}, bf16[1,1024,256]{2,1,0:T(8,128)(2,1)}, u32[]{:S(2)}, u32[]{:S(2)}) collective-permute-start(bf16[1,1024,256]{2,1,0:T(8,128)(2,1)} %collective-permute-done.1.refs_1_), channel_id=1, source_target_pairs={{0,16},{8,24},{16,0},{24,8},{1,17},{9,25},{17,1},{25,9},{2,18},{10... | collective-permute-start | bytes 1572872 | tf_op jit(solution)/shard_map/ppermute | solution.py:20
  49.8 27.2 %collective-permute-start.11 = (bf16[128,7168]{1,0:T(8,128)(2,1)S(1)}, bf16[128,7168]{1,0:T(8,128)(2,1)S(1)}, u32[]{:S(2)}, u32[]{:S(2)}) collective-permute-start(bf16[128,7168]{1,0:T(8,128)(2,1)S(1)} %broadcast_select_fusion.refs_2_), channel_id=1, source_target_pairs={{0,1},{1,0},{2,3},{3,2},{4,5},{5,4},{6,7},{7,6},{8,9},{9,8},{10,11... | collective-permute-start | bytes 5505032 | tf_op jit(solution)/shard_map/ppermute | solution.py:20
  50.9 22.1 %collective-permute-start.6 = (bf16[1024,256]{1,0:T(8,128)(2,1)S(1)}, bf16[1024,256]{1,0:T(8,128)(2,1)S(1)}, u32[]{:S(2)}, u32[]{:S(2)}) collective-permute-start(bf16[1024,256]{1,0:T(8,128)(2,1)S(1)} %get-tuple-element.61), channel_id=1, source_target_pairs={{0,2},{1,3},{2,0},{3,1},{4,6},{5,7},{6,4},{7,5},{8,10},{9,11},{10,... | collective-permute-start | bytes 1572872 | tf_op jit(solution)/shard_map/ppermute | solution.py:20
  52.2 20.7 %collective-permute-start.7 = (bf16[704,256]{1,0:T(8,128)(2,1)S(1)}, bf16[704,256]{1,0:T(8,128)(2,1)S(1)}, u32[]{:S(2)}, u32[]{:S(2)}) collective-permute-start(bf16[704,256]{1,0:T(8,128)(2,1)S(1)} %get-tuple-element.63), channel_id=1, source_target_pairs={{0,4},{1,5},{2,6},{3,7},{4,0},{5,1},{6,2},{7,3},{8,12},{9,13},{10,... | collective-permute-start | bytes 1081352 | tf_op jit(solution)/shard_map/ppermute | solution.py:20
  73.0 31.1 %collective-permute-start.8 = (bf16[1,1024,256]{2,1,0:T(8,128)(2,1)S(1)}, bf16[1,1024,256]{2,1,0:T(8,128)(2,1)S(1)}, u32[]{:S(2)}, u32[]{:S(2)}) collective-permute-start(bf16[1,1024,256]{2,1,0:T(8,128)(2,1)S(1)} %bitcast.26), channel_id=1, source_target_pairs={{0,8},{8,0},{16,24},{24,16},{1,9},{9,1},{17,25},{25,17},{2,10},{10... | collective-permute-start | bytes 1572872 | tf_op jit(solution)/shard_map/ppermute | solution.py:20
  73.9 30.1 %collective-permute-start.9 = (bf16[1,1024,256]{2,1,0:T(8,128)(2,1)S(1)}, bf16[1,1024,256]{2,1,0:T(8,128)(2,1)S(1)}, u32[]{:S(2)}, u32[]{:S(2)}) collective-permute-start(bf16[1,1024,256]{2,1,0:T(8,128)(2,1)S(1)} %bitcast.27), channel_id=1, source_target_pairs={{0,16},{8,24},{16,0},{24,8},{1,17},{9,25},{17,1},{25,9},{2,18},{10... | collective-permute-start | bytes 1572872 | tf_op jit(solution)/shard_map/ppermute | solution.py:20
  75.4 28.5 %collective-permute-start.12 = (bf16[704,256]{1,0:T(8,128)(2,1)S(1)}, bf16[704,256]{1,0:T(8,128)(2,1)S(1)}, u32[]{:S(2)}, u32[]{:S(2)}) collective-permute-start(bf16[704,256]{1,0:T(8,128)(2,1)S(1)} %get-tuple-element.73), channel_id=1, source_target_pairs={{0,6},{1,7},{2,4},{3,5},{4,2},{5,3},{6,0},{7,1},{8,14},{9,15},{10,... | collective-permute-start | bytes 1081352 | tf_op jit(solution)/shard_map/ppermute | solution.py:20
  104.1 33.1 %collective-permute-start.18 = (bf16[3,704,256]{2,1,0:T(8,128)(2,1)S(1)}, bf16[3,704,256]{2,1,0:T(8,128)(2,1)S(1)}, u32[]{:S(2)}, u32[]{:S(2)}) collective-permute-start(bf16[3,704,256]{2,1,0:T(8,128)(2,1)S(1)} %pad_maximum_fusion.1.refs_8_), channel_id=1, source_target_pairs={{0,8},{8,0},{16,24},{24,16},{1,9},{9,1},{17,25},{25,17},{2,10},{10... | collective-permute-start | bytes 3244040 | tf_op jit(solution)/shard_map/ppermute | solution.py:20
  106.8 30.4 %collective-permute-start.19 = (bf16[3,704,256]{2,1,0:T(8,128)(2,1)S(1)}, bf16[3,704,256]{2,1,0:T(8,128)(2,1)S(1)}, u32[]{:S(2)}, u32[]{:S(2)}) collective-permute-start(bf16[3,704,256]{2,1,0:T(8,128)(2,1)S(1)} %pad_maximum_fusion.1.refs_8_), channel_id=1, source_target_pairs={{0,16},{8,24},{16,0},{24,8},{1,17},{9,25},{17,1},{25,9},{2,18},{10... | collective-permute-start | bytes 3244040 | tf_op jit(solution)/shard_map/ppermute | solution.py:20
  107.2 12.0 %collective-permute-start.15 = (bf16[704,256]{1,0:T(8,128)(2,1)S(1)}, bf16[704,256]{1,0:T(8,128)(2,1)S(1)}, u32[]{:S(2)}, u32[]{:S(2)}) collective-permute-start(bf16[704,256]{1,0:T(8,128)(2,1)S(1)} %get-tuple-element.78), channel_id=1, source_target_pairs={{0,6},{1,7},{2,4},{3,5},{4,2},{5,3},{6,0},{7,1},{8,14},{9,15},{10,... | collective-permute-start | bytes 1081352 | tf_op jit(solution)/shard_map/ppermute | solution.py:20
  107.2 29.9 %collective-permute-start.10 = (bf16[1,1024,256]{2,1,0:T(8,128)(2,1)S(1)}, bf16[1,1024,256]{2,1,0:T(8,128)(2,1)S(1)}, u32[]{:S(2)}, u32[]{:S(2)}) collective-permute-start(bf16[1,1024,256]{2,1,0:T(8,128)(2,1)S(1)} %collective-permute-done.9.refs_6_), channel_id=1, source_target_pairs={{0,8},{8,0},{16,24},{24,16},{1,9},{9,1},{17,25},{25,17},{2,10},{10... | collective-permute-start | bytes 1572872 | tf_op jit(solution)/shard_map/ppermute | solution.py:20
  108.8 13.4 %collective-permute-start.14 = (bf16[704,256]{1,0:T(8,128)(2,1)S(1)}, bf16[704,256]{1,0:T(8,128)(2,1)S(1)}, u32[]{:S(2)}, u32[]{:S(2)}) collective-permute-start(bf16[704,256]{1,0:T(8,128)(2,1)S(1)} %get-tuple-element.76), channel_id=1, source_target_pairs={{0,4},{1,5},{2,6},{3,7},{4,0},{5,1},{6,2},{7,3},{8,12},{9,13},{10,... | collective-permute-start | bytes 1081352 | tf_op jit(solution)/shard_map/ppermute | solution.py:20
  119.2 9.6 %collective-permute-start.13 = (bf16[704,256]{1,0:T(8,128)(2,1)S(1)}, bf16[704,256]{1,0:T(8,128)(2,1)S(1)}, u32[]{:S(2)}, u32[]{:S(2)}) collective-permute-start(bf16[704,256]{1,0:T(8,128)(2,1)S(1)} %get-tuple-element.74), channel_id=1, source_target_pairs={{0,2},{1,3},{2,0},{3,1},{4,6},{5,7},{6,4},{7,5},{8,10},{9,11},{10,... | collective-permute-start | bytes 1081352 | tf_op jit(solution)/shard_map/ppermute | solution.py:20
  137.2 26.0 %collective-permute-start.20 = (bf16[3,704,256]{2,1,0:T(8,128)(2,1)S(1)}, bf16[3,704,256]{2,1,0:T(8,128)(2,1)}, u32[]{:S(2)}, u32[]{:S(2)}) collective-permute-start(bf16[3,704,256]{2,1,0:T(8,128)(2,1)S(1)} %pad_maximum_fusion.refs_12_), channel_id=1, source_target_pairs={{0,16},{8,24},{16,0},{24,8},{1,17},{9,25},{17,1},{25,9},{2,18},{10... | collective-permute-start | bytes 3244040 | tf_op jit(solution)/shard_map/ppermute | solution.py:20
  137.2 25.9 %collective-permute-start.21 = (bf16[3,704,256]{2,1,0:T(8,128)(2,1)S(1)}, bf16[3,704,256]{2,1,0:T(8,128)(2,1)S(1)}, u32[]{:S(2)}, u32[]{:S(2)}) collective-permute-start(bf16[3,704,256]{2,1,0:T(8,128)(2,1)S(1)} %pad_maximum_fusion.refs_12_), channel_id=1, source_target_pairs={{0,8},{8,0},{16,24},{24,16},{1,9},{9,1},{17,25},{25,17},{2,10},{10... | collective-permute-start | bytes 3244040 | tf_op jit(solution)/shard_map/ppermute | solution.py:20
  139.4 7.2 %collective-permute-start.16 = (bf16[320,256]{1,0:T(8,128)(2,1)S(1)}, bf16[320,256]{1,0:T(8,128)(2,1)S(1)}, u32[]{:S(2)}, u32[]{:S(2)}) collective-permute-start(bf16[320,256]{1,0:T(8,128)(2,1)S(1)} %get-tuple-element.79), channel_id=1, source_target_pairs={{0,4},{1,5},{2,6},{3,7},{4,0},{5,1},{6,2},{7,3},{8,12},{9,13},{10,... | collective-permute-start | bytes 491528 | tf_op jit(solution)/shard_map/ppermute | solution.py:20
  139.4 9.6 %collective-permute-start.17 = (bf16[320,256]{1,0:T(8,128)(2,1)S(1)}, bf16[320,256]{1,0:T(8,128)(2,1)S(1)}, u32[]{:S(2)}, u32[]{:S(2)}) collective-permute-start(bf16[320,256]{1,0:T(8,128)(2,1)S(1)} %get-tuple-element.81), channel_id=1, source_target_pairs={{0,6},{1,7},{2,4},{3,5},{4,2},{5,3},{6,0},{7,1},{8,14},{9,15},{10,... | collective-permute-start | bytes 491528 | tf_op jit(solution)/shard_map/ppermute | solution.py:20
  139.4 39.4 %collective-permute-start.24 = (bf16[3,704,256]{2,1,0:T(8,128)(2,1)S(1)}, bf16[3,704,256]{2,1,0:T(8,128)(2,1)S(1)}, u32[]{:S(2)}, u32[]{:S(2)}) collective-permute-start(bf16[3,704,256]{2,1,0:T(8,128)(2,1)S(1)} %collective-permute-done.18.refs_9_), channel_id=1, source_target_pairs={{0,16},{8,24},{16,0},{24,8},{1,17},{9,25},{17,1},{25,9},{2,18},{10... | collective-permute-start | bytes 3244040 | tf_op jit(solution)/shard_map/ppermute | solution.py:20
  149.0 8.8 %collective-permute-start.27 = (bf16[320,256]{1,0:T(8,128)(2,1)S(1)}, bf16[320,256]{1,0:T(8,128)(2,1)S(1)}, u32[]{:S(2)}, u32[]{:S(2)}) collective-permute-start(bf16[320,256]{1,0:T(8,128)(2,1)S(1)} %get-tuple-element.92), channel_id=1, source_target_pairs={{0,6},{1,7},{2,4},{3,5},{4,2},{5,3},{6,0},{7,1},{8,14},{9,15},{10,... | collective-permute-start | bytes 491528 | tf_op jit(solution)/shard_map/ppermute | solution.py:20
  150.0 8.1 %collective-permute-start.26 = (bf16[320,256]{1,0:T(8,128)(2,1)S(1)}, bf16[320,256]{1,0:T(8,128)(2,1)S(1)}, u32[]{:S(2)}, u32[]{:S(2)}) collective-permute-start(bf16[320,256]{1,0:T(8,128)(2,1)S(1)} %get-tuple-element.90), channel_id=1, source_target_pairs={{0,4},{1,5},{2,6},{3,7},{4,0},{5,1},{6,2},{7,3},{8,12},{9,13},{10,... | collective-permute-start | bytes 491528 | tf_op jit(solution)/shard_map/ppermute | solution.py:20
  163.2 23.2 %collective-permute-start.28 = (bf16[3,704,256]{2,1,0:T(8,128)(2,1)}, bf16[3,704,256]{2,1,0:T(8,128)(2,1)}, u32[]{:S(2)}, u32[]{:S(2)}) collective-permute-start(bf16[3,704,256]{2,1,0:T(8,128)(2,1)} %collective-permute-done.20.refs_14_), channel_id=1, source_target_pairs={{0,8},{8,0},{16,24},{24,16},{1,9},{9,1},{17,25},{25,17},{2,10},{10... | collective-permute-start | bytes 3244040 | tf_op jit(solution)/shard_map/ppermute | solution.py:20
  164.3 38.5 %collective-permute-start.30 = (bf16[3,320,256]{2,1,0:T(8,128)(2,1)S(1)}, bf16[3,320,256]{2,1,0:T(8,128)(2,1)S(1)}, u32[]{:S(2)}, u32[]{:S(2)}) collective-permute-start(bf16[3,320,256]{2,1,0:T(8,128)(2,1)S(1)} %pad_maximum_fusion.3.refs_12_), channel_id=1, source_target_pairs={{0,8},{8,0},{16,24},{24,16},{1,9},{9,1},{17,25},{25,17},{2,10},{10... | collective-permute-start | bytes 1474568 | tf_op jit(solution)/shard_map/ppermute | solution.py:20
  165.5 37.2 %collective-permute-start.31 = (bf16[3,320,256]{2,1,0:T(8,128)(2,1)S(1)}, bf16[3,320,256]{2,1,0:T(8,128)(2,1)S(1)}, u32[]{:S(2)}, u32[]{:S(2)}) collective-permute-start(bf16[3,320,256]{2,1,0:T(8,128)(2,1)S(1)} %pad_maximum_fusion.3.refs_12_), channel_id=1, source_target_pairs={{0,16},{8,24},{16,0},{24,8},{1,17},{9,25},{17,1},{25,9},{2,18},{10... | collective-permute-start | bytes 1474568 | tf_op jit(solution)/shard_map/ppermute | solution.py:20
  166.7 36.1 %collective-permute-start.22 = (bf16[3,320,256]{2,1,0:T(8,128)(2,1)S(1)}, bf16[3,320,256]{2,1,0:T(8,128)(2,1)}, u32[]{:S(2)}, u32[]{:S(2)}) collective-permute-start(bf16[3,320,256]{2,1,0:T(8,128)(2,1)S(1)} %pad_maximum_fusion.2.refs_8_), channel_id=1, source_target_pairs={{0,8},{8,0},{16,24},{24,16},{1,9},{9,1},{17,25},{25,17},{2,10},{10... | collective-permute-start | bytes 1474568 | tf_op jit(solution)/shard_map/ppermute | solution.py:20
  179.9 22.9 %collective-permute-start.23 = (bf16[3,320,256]{2,1,0:T(8,128)(2,1)S(1)}, bf16[3,320,256]{2,1,0:T(8,128)(2,1)}, u32[]{:S(2)}, u32[]{:S(2)}) collective-permute-start(bf16[3,320,256]{2,1,0:T(8,128)(2,1)S(1)} %pad_maximum_fusion.2.refs_8_), channel_id=1, source_target_pairs={{0,16},{8,24},{16,0},{24,8},{1,17},{9,25},{17,1},{25,9},{2,18},{10... | collective-permute-start | bytes 1474568 | tf_op jit(solution)/shard_map/ppermute | solution.py:20
  202.8 17.9 %collective-permute-start.32 = (bf16[3,320,256]{2,1,0:T(8,128)(2,1)S(1)}, bf16[3,320,256]{2,1,0:T(8,128)(2,1)S(1)}, u32[]{:S(2)}, u32[]{:S(2)}) collective-permute-start(bf16[3,320,256]{2,1,0:T(8,128)(2,1)S(1)} %collective-permute-done.31.refs_14_), channel_id=1, source_target_pairs={{0,8},{8,0},{16,24},{24,16},{1,9},{9,1},{17,25},{25,17},{2,10},{10... | collective-permute-start | bytes 1474568 | tf_op jit(solution)/shard_map/ppermute | solution.py:20
  205.0 15.8 %collective-permute-start.29 = (bf16[3,320,256]{2,1,0:T(8,128)(2,1)}, bf16[3,320,256]{2,1,0:T(8,128)(2,1)S(1)}, u32[]{:S(2)}, u32[]{:S(2)}) collective-permute-start(bf16[3,320,256]{2,1,0:T(8,128)(2,1)} %collective-permute-done.22.refs_9_), channel_id=1, source_target_pairs={{0,16},{8,24},{16,0},{24,8},{1,17},{9,25},{17,1},{25,9},{2,18},{10... | collective-permute-start | bytes 1474568 | tf_op jit(solution)/shard_map/ppermute | solution.py:20
  (22 other events, 566.8 us)

commit v2 on v1

--- a/solution.py
+++ b/solution.py
@@ -8,8 +8,7 @@
 from jax.experimental.pallas import tpu as pltpu
 from jax.sharding import PartitionSpec as P
 
-BOUNDS = (0, 11, 16)
-CALLS = ((0, 6, 11), (11, 16))
+BOUNDS = (0, 6, 11, 16)
 ROW_STEPS = 4
 PAIRS = 2
 FOLD_VMEM = 28 * 1024 * 1024
@@ -40,7 +39,7 @@
 
 
 def spectra_kernel(late, cuts, scale, core_ref, weights_ref, table_ref, *refs):
-    sources = 4 if late else 2
+    sources = 6 if late else 2
     inputs, outs = refs[:sources], refs[sources:-4]
     samples, folded, spread, sems = refs[-4:]
     core = core_ref[0]
@@ -59,12 +58,13 @@
             sems.at[which, step],
         )
 
-    def halo_copy(ref, step):
+    def halo_copy(refs, step, which):
         rows = pl.ds(step * step_rows, step_rows)
+        start = slab + which * refs[0].shape[1]
         return pltpu.make_async_copy(
-            ref.at[pl.ds(step * step_rows % half_rows, step_rows), :],
-            samples.at[rows, pl.ds(slab, tail)],
-            sems.at[1, step],
+            refs[which].at[pl.ds(step * step_rows % half_rows, step_rows), :],
+            samples.at[rows, pl.ds(start, refs[which].shape[1])],
+            sems.at[1 + which, step],
         )
 
     def start_all(first, second):
@@ -89,16 +89,19 @@
 
             @pl.when(core == half)
             def _():
-                halo_copy(inputs[2], step).start()
+                halo_copy(inputs[2:4], step, 0).start()
+                halo_copy(inputs[2:4], step, 1).start()
 
             @pl.when(core != half)
             def _():
-                halo_copy(inputs[3], step).start()
+                halo_copy(inputs[4:6], step, 0).start()
+                halo_copy(inputs[4:6], step, 1).start()
 
     for step in range(ROW_STEPS):
         slab_copy(own, step, slab, 0, 0).wait()
         if late:
-            halo_copy(inputs[2], step).wait()
+            halo_copy(inputs[2:4], step, 0).wait()
+            halo_copy(inputs[2:4], step, 1).wait()
         else:
             slab_copy(own, step, tail, slab, 1).wait()
 
@@ -161,7 +164,7 @@
             pltpu.VMEM((count, (frames + depth - 1) * width), jnp.bfloat16),
             pltpu.VMEM((frames, count, width), jnp.bfloat16),
             pltpu.VMEM((count // 128, channels * frames, 128), jnp.float32),
-            pltpu.SemaphoreType.DMA((2, ROW_STEPS)),
+            pltpu.SemaphoreType.DMA((3, ROW_STEPS)),
         ],
         compiler_params=pltpu.CompilerParams(vmem_limit_bytes=FOLD_VMEM),
         cost_estimate=pl.CostEstimate(flops=1, bytes_accessed=1, transcendentals=0),
@@ -195,8 +198,8 @@
 
     depth = len(pieces) * 16
     places = lax.broadcasted_iota(jnp.int32, (count, depth), 1)
-    even = jnp.where(places % 16 < 8, scale, 0.0).astype(jnp.bfloat16)
-    odd = jnp.where(places % 16 < 8, 0.0, scale).astype(jnp.bfloat16)
+    even = jnp.where(places % 16 < 8, 1.0, 0.0).astype(jnp.bfloat16)
+    odd = jnp.where(places % 16 < 8, 0.0, 1.0).astype(jnp.bfloat16)
     for pair in range(PAIRS):
         rows = slice(pair * 16, pair * 16 + 16)
 
@@ -214,7 +217,7 @@
         turned = stack(0).T
         left = jnp.concatenate([turned * even, turned * odd], axis=0)
         for member in range(groups):
-            summed = lax.dot_general(
+            summed = scale * lax.dot_general(
                 left, stack(member), (((1,), (0,)), ((), ())), preferred_element_type=jnp.float32
             )
             columns = pl.ds(pl.multiple_of((group ^ member) * count, 128), count)
@@ -233,13 +236,11 @@
         wait_all(1 - slot)
 
 
-def correlate(frames, first, stop, start, channels, group, wide, narrow, earlier):
+def correlate(frames, first, stop, channels, group, wide, narrow, earlier):
     groups, count = lax.axis_size("grp"), (wide + narrow)[0][-1].shape[-1]
     block = 2 * PAIRS
     base, steps = first // block, (stop - first) // block
-    pieces = [(piece, base) for piece in wide] + [
-        (piece, (first - start) // block) for piece in narrow
-    ]
+    pieces = [(piece, base) for piece in wide] + [(piece, 0) for piece in narrow]
     ordered = [len(piece) == 1 for piece, _ in pieces]
     operands = [array for piece, _ in pieces for array in piece]
     aliases = {} if earlier is None else {1 + len(operands): 0}
@@ -273,19 +274,17 @@
     )(group, *operands, *carried)
 
 
-def joined(block, turn, earlier=(), events=()):
+def joined(block, turn, earlier=None, events=()):
     groups = lax.axis_size("grp")
     bits = [1 << b for b in range(groups.bit_length() - 1)]
     bits = bits[turn % len(bits) :] + bits[: turn % len(bits)]
-    held = {bit: swap(after(block, *earlier), "grp", bit) for bit in bits}
-    direct = tuple(held[bit] for bit in bits)
-    reached = bits[:1]
-    for bit in bits[1:]:
-        for member in list(reached):
-            held[member | bit] = swap(after(held[member], *direct, *events), "grp", bit)
-        reached += [bit] + [member | bit for member in reached]
-    held[0] = block
-    return [held[member] for member in range(groups)], direct
+    held = {0: block}
+    for bit in bits:
+        for member in list(held):
+            waits = () if earlier is None else (earlier[member | bit],)
+            sent = after(held[member], *waits, *(events if member else ()))
+            held[member | bit] = swap(sent, "grp", bit)
+    return [held[member] for member in range(groups)]
 
 
 def on_device(voltages, prototype):
@@ -303,9 +302,21 @@
     other = swap(voltages, "chan", 1)
     route = [[(2 * p + 2, 2 * p + k) for p in range(parts - 1)] for k in (0, 1)]
     tail = (depth - 1) * width
-    sliced = [voltages[k * half : k * half + half, :tail] for k in (0, 1)]
-    ahead = [lax.ppermute(sliced[k], "chan", route[k]) for k in (0, 1)]
-    other = after(other, *sliced)
+    split = width * ((depth - 1) // 2)
+
+    def ahead_of(first, stop, *events):
+        return [
+            lax.ppermute(
+                after(voltages[k * half : k * half + half, first:stop], *events), "chan", route[k]
+            )
+            for k in (0, 1)
+        ]
+
+    def swapped(pair):
+        mine = jnp.where(core == 0, pair[0], pair[1])
+        return mine, swap(mine, "chan", 1)
+
+    ahead = ahead_of(0, split)
 
     owned = (place // 2) ^ jnp.arange(parts, dtype=jnp.int32)
     table = cosine_rows((owned * 2 + core) * channels, channels, width)
@@ -313,70 +324,44 @@
     weights = signs[:, None] * prototype
     at_core = core.reshape(1)
 
+    cuts = [(part * channels, channels) for part in range(parts)]
+    early = spectra_blocks(False, cuts, at_core, weights, table, [voltages, other])
+    own_early = joined(early[0][None], 0)
+    near = swap(after(early[1], *ahead), "chan", 2)
+    middle = swap(after(early[2], *ahead), "chan", 4)
+    near_joined = joined(near[None], 1, own_early)
+    middle_joined = joined(middle[None], 0, near_joined)
+    rest = ahead_of(split, tail, near, middle, *own_early[1:3])
+    far = [swap(after(early[part], *rest), "chan", 2 * part) for part in range(3, parts)]
+    halo, other_halo = swapped(ahead)
+    rest = lax.optimization_barrier((*rest, *middle_joined[1:3]))[:2]
+    halo_rest, other_rest = swapped(rest)
+    sources = [voltages, other, halo, halo_rest, other_halo, other_rest]
     bounds = [round(channels * bound / 64) * 4 for bound in BOUNDS]
     blocks = list(zip(bounds[:-1], bounds[1:]))
-    cuts = [(0, channels), (channels, channels)] + [
-        (part * channels + first, stop - first) for first, stop in blocks for part in range(2, parts)
+    cuts = [(0, channels)] + [
+        (part * channels + first, stop - first)
+        for first, stop in blocks
+        for part in range(1, parts)
     ]
-    early = spectra_blocks(False, cuts, at_core, weights, table, [voltages, other])
-    own_early, sent = joined(early[0][None], 0)
-    ahead = lax.optimization_barrier((ahead[0], ahead[1], *own_early[1:]))
-    halo = jnp.where(core == 0, ahead[0], ahead[1])
-    other_halo = swap(halo, "chan", 1)
-
-    near = swap(after(early[1], ahead[0], ahead[1]), "chan", 2)
-    early_parts = [early[2 + i * (parts - 2) :][: parts - 2] for i in range(len(blocks))]
-    middle = swap(after(early_parts[0][0], ahead[0], ahead[1]), "chan", 4)
-    near, middle = lax.optimization_barrier((near, middle))
-    near_joined, sent = joined(near[None], 1, sent)
-
-    cuts = [(first, stop - first) for first, stop in blocks] + [
-        (part * channels + first, stop - first) for first, stop in blocks for part in range(1, parts)
-    ]
-    late = spectra_blocks(
-        True, cuts, at_core, weights, table, [voltages, other, halo, after(other_halo, near)]
-    )
-    moved, landed = [], ()
-    for index in range(len(blocks)):
-        if index > 0:
-            middle = swap(after(early_parts[index][0], *landed), "chan", 4)
-        waits = (middle,) if index == 0 else landed
-        far = [
-            swap(after(early_parts[index][part - 2], *waits), "chan", 2 * part)
-            for part in range(3, parts)
-        ]
-        late_parts = late[len(blocks) + index * (parts - 1) :][: parts - 1]
-        hops = [
-            swap(after(late_parts[part - 1], middle, *far), "chan", 2 * part)
+    late = spectra_blocks(True, cuts, at_core, weights, table, sources)
+    own_late = joined(late[0][None], 1, middle_joined)
+    far_joined = joined(jnp.stack(far), 0, own_late)
+    wide = [own_early, near_joined, middle_joined, own_late, far_joined]
+    landed, narrow, results = [near, middle] + far, [far_joined], [None]
+    for chunk, (first, stop) in enumerate(blocks):
+        skipped = chunk * (parts - 1)
+        landed = [
+            swap(after(late[skipped + part], landed[part - 1]), "chan", 2 * part)
             for part in range(1, parts)
         ]
-        landed = tuple(hops)
-        moved.append((jnp.stack([late[index], middle] + far), jnp.stack(hops)))
-
-    wide, results = [own_early, near_joined], [None]
-    for index, (first, stop) in enumerate(blocks):
-        ready, own_sent = joined(moved[index][0], 0, sent, results[1:2])
-        if index == 0:
-            sent = own_sent + tuple(near_joined[1:])
-        rest, own_sent = joined(
-            moved[index][1], 1, sent, results[1:2] if index > 0 else landed
+        events = results[chunk - 1 : chunk] if chunk >= 2 else ()
+        narrow.append(joined(jnp.stack(landed), chunk + 1, narrow[-1], events))
+        results.append(
+            correlate(
+                frames, first, stop, channels, group.reshape(1), wide, [narrow[-1]], results[-1]
+            )
         )
-        sent = own_sent
-        calls = [round(channels * bound / 64) * 4 for bound in CALLS[index]]
-        for call_first, call_stop in zip(calls[:-1], calls[1:]):
-            results.append(
-                correlate(
-                    frames,
-                    call_first,
-                    call_stop,
-                    first,
-                    channels,
-                    group.reshape(1),
-                    wide,
-                    [ready, rest],
-                    results[-1],
-                )
-            )
     return results[-1]
 
 

time: 240 us -> 239 us (level)
  waiting for transfers between devices: 121 us -> 106 us
  starting transfers between devices: 38.9 us -> 52.2 us
    ppermute x2 -> x4, waiting for transfers between devices: 8.76 us -> 0.35 us  [ahead_of(): lax.ppermute(after(voltages[k * half:k * half + half, first:stop], *event...]
    ppermute x31 -> x39, starting transfers between devices: 33.2 us -> 40.8 us  [swap(): lax.ppermute(block, axis, [(i, i ^ bit) for i in range(lax.axis_size(axis...]
    ppermute x31 -> x39, waiting for transfers between devices: 112 us -> 106 us  [swap(): lax.ppermute(block, axis, [(i, i ^ bit) for i in range(lax.axis_size(axis...]
    ppermute x2 -> x4, starting transfers between devices: 5.7 us -> 11.4 us  [ahead_of(): lax.ppermute(after(voltages[k * half:k * half + half, first:stop], *event...]
    unnamed x42 -> x56, local copies, waits for them, and re-layouts: 5.67 us -> 5.83 us
  transfers between devices with their start and end apart: 33 -> 43, of which waited for: 17 -> 17; matrix products, arithmetic and copies ran while one was open for 3% -> 4% of each run, Pallas kernels for 21% -> 20%
where the time goes in v2:
time: 239 us; the launch traced here: 236 us
  waiting for transfers between devices  106 us (44%)
  Pallas kernels  61.3 us (26%)
  starting transfers between devices  52.2 us (22%)
  local copies, waits for them, and re-layouts  10 us (4%)
  other arithmetic  5.68 us (2%)
    ppermute x39, waiting for transfers between devices, swap(): lax.ppermute(block, axis, [(i, i ^ bit) for i in range(lax.axis_size(axis...  106 us
    pallas_call x3, Pallas kernels, correlate(): pl.pallas_call(functools.partial(correlate_kernel, 1.0 / frames, groups,...  42.4 us
    ppermute x39, starting transfers between devices, swap(): lax.ppermute(block, axis, [(i, i ^ bit) for i in range(lax.axis_size(axis...  40.8 us
    pallas_call x2, Pallas kernels, spectra_blocks(): pl.pallas_call(functools.partial(spectra_kernel, late, cuts, math.sqrt(2....  18.8 us
    ppermute x4, starting transfers between devices, ahead_of(): lax.ppermute(after(voltages[k * half:k * half + half, first:stop], *event...  11.4 us
    unnamed x56, local copies, waits for them, and re-layouts  5.83 us
  transfers between devices with their start and end apart: 43, of which 17 were waited for; matrix products, arithmetic and copies ran while one was open for 4% of the time, Pallas kernels for 20%

profile of v2, /device:TPU:16, one launch (start us, length us, event | category | flops | bytes accessed | tf_op | source)
XLA Modules:
  0.0 235.7 jit_solution(2274190695160249745)
XLA Ops:
  0.0 2.6 %fusion.11 = (bf16[128,3072]{1,0:T(8,128)(2,1)}, bf16[128,3072]{1,0:T(8,128)(2,1)}) fusion(bf16[256,8192]{1,0:T(8,128)(2,1)} %refs_0_.3), kind=kLoop, calls=%fused_computation.35 | loop fusion | bytes 3145728 | tf_op jit(solution)/shard_map/slice | solution.py:310
  2.6 2.3 collective-permute-start.4
  5.0 2.6 %collective-permute-start.5 = (bf16[128,3072]{1,0:T(8,128)(2,1)}, bf16[128,3072]{1,0:T(8,128)(2,1)}, u32[]{:S(2)}, u32[]{:S(2)}) collective-permute-start(bf16[128,3072]{1,0:T(8,128)(2,1)} %get-tuple-element.117), channel_id=1, source_target_pairs={{2,1},{4,3},{6,5},{10,9},{12,11},{14,13},{18,17},{20,19},{22,21},{... | collective-permute-start | bytes 2359304 | tf_op jit(solution)/shard_map/ppermute | solution.py:309
  9.8 2.2 copy-done
  12.0 9.4 %fold_transform.2 = (bf16[1024,256]{1,0:T(8,128)(2,1)S(1)}, bf16[1024,256]{1,0:T(8,128)(2,1)S(1)}, bf16[1024,256]{1,0:T(8,128)(2,1)S(1)}, bf16[1024,256]{1,0:T(8,128)(2,1)S(1)}) custom-call(s32[1]{0:T(128)} %bitcast.1.core_ref, f32[8,1024]{1,0:T(8,128)S(1)} %broadcast_multiply_fusion.weights_ref, bf16[512,1024]{1,0:T(8,128)(2,1)S(1)} %bitcast.17, ...), custom_call_target="tpu_custom_call" | custom-call | flops 1 | bytes 1 | tf_op jit(solution)/shard_map/fold_transform/pallas_call | solution.py:157
  24.5 2.2 collective-permute-start.6
  28.2 22.1 %collective-permute-done.6 = bf16[1024,256]{1,0:T(8,128)(2,1)S(1)} collective-permute-done((bf16[1024,256]{1,0:T(8,128)(2,1)S(1)}, bf16[1024,256]{1,0:T(8,128)(2,1)S(1)}, u32[]{:S(2)}, u32[]{:S(2)}) %collective-permute-start.6) | collective-permute-done | bytes 524320 | tf_op jit(solution)/shard_map/ppermute | solution.py:19
  51.5 4.1 %collective-permute-start.15 = (bf16[128,4096]{1,0:T(8,128)(2,1)}, bf16[128,4096]{1,0:T(8,128)(2,1)}, u32[]{:S(2)}, u32[]{:S(2)}) collective-permute-start(bf16[128,4096]{1,0:T(8,128)(2,1)} %get-tuple-element.76), channel_id=1, source_target_pairs={{2,1},{4,3},{6,5},{10,9},{12,11},{14,13},{18,17},{20,19},{22,21},{... | collective-permute-start | bytes 3145736 | tf_op jit(solution)/shard_map/ppermute | solution.py:309
  55.6 2.4 %collective-permute-start.14 = (bf16[128,4096]{1,0:T(8,128)(2,1)}, bf16[128,4096]{1,0:T(8,128)(2,1)}, u32[]{:S(2)}, u32[]{:S(2)}) collective-permute-start(bf16[128,4096]{1,0:T(8,128)(2,1)} %get-tuple-element.75), channel_id=1, source_target_pairs={{2,0},{4,2},{6,4},{10,8},{12,10},{14,12},{18,16},{20,18},{22,20},{... | collective-permute-start | bytes 3145736 | tf_op jit(solution)/shard_map/ppermute | solution.py:309
  58.1 5.8 %collective-permute-done.8.refs_6_ = bf16[1,1024,256]{2,1,0:T(8,128)(2,1)S(1)} collective-permute-done((bf16[1,1024,256]{2,1,0:T(8,128)(2,1)S(1)}, bf16[1,1024,256]{2,1,0:T(8,128)(2,1)S(1)}, u32[]{:S(2)}, u32[]{:S(2)}) %collective-permute-start.8) | collective-permute-done | bytes 524320 | tf_op jit(solution)/shard_map/ppermute | solution.py:19
  67.7 11.3 %collective-permute-done.12.refs_10_ = bf16[1,1024,256]{2,1,0:T(8,128)(2,1)} collective-permute-done((bf16[1,1024,256]{2,1,0:T(8,128)(2,1)}, bf16[1,1024,256]{2,1,0:T(8,128)(2,1)}, u32[]{:S(2)}, u32[]{:S(2)}) %collective-permute-start.12) | collective-permute-done | bytes 524320 | tf_op jit(solution)/shard_map/ppermute | solution.py:19
  82.6 5.4 %collective-permute-done.3.refs_3_ = bf16[1,1024,256]{2,1,0:T(8,128)(2,1)S(1)} collective-permute-done((bf16[1,1024,256]{2,1,0:T(8,128)(2,1)S(1)}, bf16[1,1024,256]{2,1,0:T(8,128)(2,1)S(1)}, u32[]{:S(2)}, u32[]{:S(2)}) %collective-permute-start.3) | collective-permute-done | bytes 524320 | tf_op jit(solution)/shard_map/ppermute | solution.py:19
  91.3 9.4 %fold_transform.3 = (bf16[1024,256]{1,0:T(8,128)(2,1)S(1)}, bf16[384,256]{1,0:T(8,128)(2,1)S(1)}, bf16[384,256]{1,0:T(8,128)(2,1)S(1)}, bf16[384,256]{1,0:T(8,12...) custom-call(s32[1]{0:T(128)} %bitcast.1.core_ref, ...), custom_call_target="tpu_custom_call" | custom-call | flops 1 | bytes 1 | tf_op jit(solution)/shard_map/fold_transform/pallas_call | solution.py:157
  103.5 9.7 %collective-permute-done.21 = bf16[1024,256]{1,0:T(8,128)(2,1)S(1)} collective-permute-done((bf16[1024,256]{1,0:T(8,128)(2,1)S(1)}, bf16[1024,256]{1,0:T(8,128)(2,1)S(1)}, u32[]{:S(2)}, u32[]{:S(2)}) %collective-permute-start.21) | collective-permute-done | bytes 524320 | tf_op jit(solution)/shard_map/ppermute | solution.py:19
  113.6 3.0 %collective-permute-done.13.refs_11_ = bf16[1,1024,256]{2,1,0:T(8,128)(2,1)S(1)} collective-permute-done((bf16[1,1024,256]{2,1,0:T(8,128)(2,1)}, bf16[1,1024,256]{2,1,0:T(8,128)(2,1)S(1)}, u32[]{:S(2)}, u32[]{:S(2)}) %collective-permute-start.13) | collective-permute-done | bytes 524320 | tf_op jit(solution)/shard_map/ppermute | solution.py:19
  116.6 7.5 %collective-permute-done.19.refs_14_ = bf16[1,1024,256]{2,1,0:T(8,128)(2,1)S(1)} collective-permute-done((bf16[1,1024,256]{2,1,0:T(8,128)(2,1)S(1)}, bf16[1,1024,256]{2,1,0:T(8,128)(2,1)S(1)}, u32[]{:S(2)}, u32[]{:S(2)}) %collective-permute-start.19) | collective-permute-done | bytes 524320 | tf_op jit(solution)/shard_map/ppermute | solution.py:19
  124.1 2.3 collective-permute-start.20
  129.2 2.9 %collective-permute-start.28 = (bf16[384,256]{1,0:T(8,128)(2,1)S(1)}, bf16[384,256]{1,0:T(8,128)(2,1)S(1)}, u32[]{:S(2)}, u32[]{:S(2)}) collective-permute-start(bf16[384,256]{1,0:T(8,128)(2,1)S(1)} %get-tuple-element.97), channel_id=1, source_target_pairs={{0,4},{1,5},{2,6},{3,7},{4,0},{5,1},{6,2},{7,3},{8,12},{9,13},{10,... | collective-permute-start | bytes 589832 | tf_op jit(solution)/shard_map/ppermute | solution.py:19
  132.1 5.5 %collective-permute-done.20.refs_15_ = bf16[1,1024,256]{2,1,0:T(8,128)(2,1)S(1)} collective-permute-done((bf16[1,1024,256]{2,1,0:T(8,128)(2,1)S(1)}, bf16[1,1024,256]{2,1,0:T(8,128)(2,1)S(1)}, u32[]{:S(2)}, u32[]{:S(2)}) %collective-permute-start.20) | collective-permute-done | bytes 524320 | tf_op jit(solution)/shard_map/ppermute | solution.py:19
  137.6 2.2 collective-permute-start.24
  141.0 4.1 %collective-permute-done.31 = bf16[384,256]{1,0:T(8,128)(2,1)S(1)} collective-permute-done((bf16[384,256]{1,0:T(8,128)(2,1)S(1)}, bf16[384,256]{1,0:T(8,128)(2,1)S(1)}, u32[]{:S(2)}, u32[]{:S(2)}) %collective-permute-start.31) | collective-permute-done | bytes 196640 | tf_op jit(solution)/shard_map/ppermute | solution.py:19
  145.9 2.6 %collective-permute-start.29 = (bf16[320,256]{1,0:T(8,128)(2,1)S(1)}, bf16[320,256]{1,0:T(8,128)(2,1)S(1)}, u32[]{:S(2)}, u32[]{:S(2)}) collective-permute-start(bf16[320,256]{1,0:T(8,128)(2,1)S(1)} %get-tuple-element.98), channel_id=1, source_target_pairs={{0,4},{1,5},{2,6},{3,7},{4,0},{5,1},{6,2},{7,3},{8,12},{9,13},{10,... | collective-permute-start | bytes 491528 | tf_op jit(solution)/shard_map/ppermute | solution.py:19
  148.5 4.1 %collective-permute-done.24.refs_19_ = bf16[1,1024,256]{2,1,0:T(8,128)(2,1)S(1)} collective-permute-done((bf16[1,1024,256]{2,1,0:T(8,128)(2,1)S(1)}, bf16[1,1024,256]{2,1,0:T(8,128)(2,1)S(1)}, u32[]{:S(2)}, u32[]{:S(2)}) %collective-permute-start.24) | collective-permute-done | bytes 524320 | tf_op jit(solution)/shard_map/ppermute | solution.py:19
  154.5 8.6 %collective-permute-done.37.refs_22_ = bf16[3,384,256]{2,1,0:T(8,128)(2,1)S(1)} collective-permute-done((bf16[3,384,256]{2,1,0:T(8,128)(2,1)S(1)}, bf16[3,384,256]{2,1,0:T(8,128)(2,1)S(1)}, u32[]{:S(2)}, u32[]{:S(2)}) %collective-permute-start.37) | collective-permute-done | bytes 589856 | tf_op jit(solution)/shard_map/ppermute | solution.py:19
  165.1 2.0 collective-permute-start.35
  168.1 5.6 %collective-permute-done.27 = bf16[320,256]{1,0:T(8,128)(2,1)S(1)} collective-permute-done((bf16[320,256]{1,0:T(8,128)(2,1)S(1)}, bf16[320,256]{1,0:T(8,128)(2,1)S(1)}, u32[]{:S(2)}, u32[]{:S(2)}) %collective-permute-start.27) | collective-permute-done | bytes 163872 | tf_op jit(solution)/shard_map/ppermute | solution.py:19
  173.7 4.3 %collective-permute-done.30 = bf16[320,256]{1,0:T(8,128)(2,1)S(1)} collective-permute-done((bf16[320,256]{1,0:T(8,128)(2,1)S(1)}, bf16[320,256]{1,0:T(8,128)(2,1)S(1)}, u32[]{:S(2)}, u32[]{:S(2)}) %collective-permute-start.30) | collective-permute-done | bytes 163872 | tf_op jit(solution)/shard_map/ppermute | solution.py:19
  178.0 3.7 %collective-permute-done.33 = bf16[320,256]{1,0:T(8,128)(2,1)S(1)} collective-permute-done((bf16[320,256]{1,0:T(8,128)(2,1)S(1)}, bf16[320,256]{1,0:T(8,128)(2,1)S(1)}, u32[]{:S(2)}, u32[]{:S(2)}) %collective-permute-start.33) | collective-permute-done | bytes 163872 | tf_op jit(solution)/shard_map/ppermute | solution.py:19
  183.3 3.7 %collective-permute-done.35.refs_21_ = bf16[3,320,256]{2,1,0:T(8,128)(2,1)} collective-permute-done((bf16[3,320,256]{2,1,0:T(8,128)(2,1)S(1)}, bf16[3,320,256]{2,1,0:T(8,128)(2,1)}, u32[]{:S(2)}, u32[]{:S(2)}) %collective-permute-start.35) | collective-permute-done | bytes 491552 | tf_op jit(solution)/shard_map/ppermute | solution.py:19
  189.7 15.7 %correlate.3.refs_24_ = bf16[128,256,1024]{2,1,0:T(8,128)(2,1)} custom-call(s32[1]{0:T(128)} %bitcast.group_ref, bf16[1,1024,256]{2,1,0:T(8,128)(2,1)} %bitcast.21, bf16[1,1024,256]{2,1,0:T(8,128)(2,1)} %copy-done.4, bf16[1,1024,256]{2,1,0:T(8,128)(2,1)} %copy-done.5, bf16[1,1024,256]{2,1,0:T(8,128)(2,1)} %copy-done.10, bf16[1,1024,256]{2,1,0:T(8,128)(2,1)} %bitcast.31, ...), custom_call_target="tpu_custom_call" | custom-call | flops 1 | bytes 1 | tf_op jit(solution)/shard_map/correlate/pallas_call | solution.py:256
  207.2 13.4 %correlate.4.refs_24_ = bf16[128,256,1024]{2,1,0:T(8,128)(2,1)} custom-call(s32[1]{0:T(128)} %bitcast.group_ref, bf16[1,1024,256]{2,1,0:T(8,128)(2,1)} %bitcast.22, bf16[1,1024,256]{2,1,0:T(8,128)(2,1)} %copy-done.4, bf16[1,1024,256]{2,1,0:T(8,128)(2,1)} %copy-done.5, bf16[1,1024,256]{2,1,0:T(8,128)(2,1)} %copy-done.10, ...), custom_call_target="tpu_custom_call", output_to_operand_aliasing={{}: (25, {})} | custom-call | flops 1 | bytes 1 | tf_op jit(solution)/shard_map/correlate/pallas_call | solution.py:256
  222.2 13.4 %correlate.5 = bf16[128,256,1024]{2,1,0:T(8,128)(2,1)} custom-call(s32[1]{0:T(128)} %bitcast.group_ref, bf16[1,1024,256]{2,1,0:T(8,128)(2,1)} %bitcast.23, bf16[1,1024,256]{2,1,0:T(8,128)(2,1)} %copy-done.4, bf16[1,1024,256]{2,1,0:T(8,128)(2,1)} %copy-done.5, bf16[1,1024,256]{2,1,0:T(8,128)(2,1)} %copy-done.10, ...), custom_call_target="tpu_custom_call", output_to_operand_aliasing={{}: (25, {})} | custom-call | flops 1 | bytes 1 | tf_op jit(solution)/shard_map/correlate/pallas_call | solution.py:256
  (133 shorter events, 39.1 us)
Async XLA Ops:
  2.6 21.9 %collective-permute-start.4 = (bf16[128,3072]{1,0:T(8,128)(2,1)}, bf16[128,3072]{1,0:T(8,128)(2,1)}, u32[]{:S(2)}, u32[]{:S(2)}) collective-permute-start(bf16[128,3072]{1,0:T(8,128)(2,1)} %get-tuple-element.118), channel_id=1, source_target_pairs={{2,0},{4,2},{6,4},{10,8},{12,10},{14,12},{18,16},{20,18},{22,20},{... | collective-permute-start | bytes 2359304 | tf_op jit(solution)/shard_map/ppermute | solution.py:309
  5.0 19.5 %collective-permute-start.5 = (bf16[128,3072]{1,0:T(8,128)(2,1)}, bf16[128,3072]{1,0:T(8,128)(2,1)}, u32[]{:S(2)}, u32[]{:S(2)}) collective-permute-start(bf16[128,3072]{1,0:T(8,128)(2,1)} %get-tuple-element.117), channel_id=1, source_target_pairs={{2,1},{4,3},{6,5},{10,9},{12,11},{14,13},{18,17},{20,19},{22,21},{... | collective-permute-start | bytes 2359304 | tf_op jit(solution)/shard_map/ppermute | solution.py:309
  21.4 29.3 %collective-permute-start.1 = (bf16[1,1024,256]{2,1,0:T(8,128)(2,1)S(1)}, bf16[1,1024,256]{2,1,0:T(8,128)(2,1)S(1)}, u32[]{:S(2)}, u32[]{:S(2)}) collective-permute-start(bf16[1,1024,256]{2,1,0:T(8,128)(2,1)S(1)} %bitcast.19), channel_id=1, source_target_pairs={{0,8},{8,0},{16,24},{24,16},{1,9},{9,1},{17,25},{25,17},{2,10},{10... | collective-permute-start | bytes 1572872 | tf_op jit(solution)/shard_map/ppermute | solution.py:19
  23.0 27.3 %collective-permute-start.2 = (bf16[1,1024,256]{2,1,0:T(8,128)(2,1)S(1)}, bf16[1,1024,256]{2,1,0:T(8,128)(2,1)S(1)}, u32[]{:S(2)}, u32[]{:S(2)}) collective-permute-start(bf16[1,1024,256]{2,1,0:T(8,128)(2,1)S(1)} %bitcast.20), channel_id=1, source_target_pairs={{0,16},{8,24},{16,0},{24,8},{1,17},{9,25},{17,1},{25,9},{2,18},{10... | collective-permute-start | bytes 1572872 | tf_op jit(solution)/shard_map/ppermute | solution.py:19
  24.5 26.2 %collective-permute-start.10 = (bf16[1024,256]{1,0:T(8,128)(2,1)S(1)}, bf16[1024,256]{1,0:T(8,128)(2,1)}, u32[]{:S(2)}, u32[]{:S(2)}) collective-permute-start(bf16[1024,256]{1,0:T(8,128)(2,1)S(1)} %get-tuple-element.71), channel_id=1, source_target_pairs={{0,4},{1,5},{2,6},{3,7},{4,0},{5,1},{6,2},{7,3},{8,12},{9,13},{10,... | collective-permute-start | bytes 1572872 | tf_op jit(solution)/shard_map/ppermute | solution.py:19
  24.5 25.7 %collective-permute-start.6 = (bf16[1024,256]{1,0:T(8,128)(2,1)S(1)}, bf16[1024,256]{1,0:T(8,128)(2,1)S(1)}, u32[]{:S(2)}, u32[]{:S(2)}) collective-permute-start(bf16[1024,256]{1,0:T(8,128)(2,1)S(1)} %get-tuple-element.66), channel_id=1, source_target_pairs={{0,2},{1,3},{2,0},{3,1},{4,6},{5,7},{6,4},{7,5},{8,10},{9,11},{10,... | collective-permute-start | bytes 1572872 | tf_op jit(solution)/shard_map/ppermute | solution.py:19
  50.2 13.7 %collective-permute-start.8 = (bf16[1,1024,256]{2,1,0:T(8,128)(2,1)S(1)}, bf16[1,1024,256]{2,1,0:T(8,128)(2,1)S(1)}, u32[]{:S(2)}, u32[]{:S(2)}) collective-permute-start(bf16[1,1024,256]{2,1,0:T(8,128)(2,1)S(1)} %bitcast.29), channel_id=1, source_target_pairs={{0,16},{8,24},{16,0},{24,8},{1,17},{9,25},{17,1},{25,9},{2,18},{10... | collective-permute-start | bytes 1572872 | tf_op jit(solution)/shard_map/ppermute | solution.py:19
  51.1 13.8 %collective-permute-start.7 = (bf16[1,1024,256]{2,1,0:T(8,128)(2,1)S(1)}, bf16[1,1024,256]{2,1,0:T(8,128)(2,1)S(1)}, u32[]{:S(2)}, u32[]{:S(2)}) collective-permute-start(bf16[1,1024,256]{2,1,0:T(8,128)(2,1)S(1)} %bitcast.30), channel_id=1, source_target_pairs={{0,8},{8,0},{16,24},{24,16},{1,9},{9,1},{17,25},{25,17},{2,10},{10... | collective-permute-start | bytes 1572872 | tf_op jit(solution)/shard_map/ppermute | solution.py:19
  51.5 27.6 %collective-permute-start.15 = (bf16[128,4096]{1,0:T(8,128)(2,1)}, bf16[128,4096]{1,0:T(8,128)(2,1)}, u32[]{:S(2)}, u32[]{:S(2)}) collective-permute-start(bf16[128,4096]{1,0:T(8,128)(2,1)} %get-tuple-element.76), channel_id=1, source_target_pairs={{2,1},{4,3},{6,5},{10,9},{12,11},{14,13},{18,17},{20,19},{22,21},{... | collective-permute-start | bytes 3145736 | tf_op jit(solution)/shard_map/ppermute | solution.py:309
  55.6 23.8 %collective-permute-start.14 = (bf16[128,4096]{1,0:T(8,128)(2,1)}, bf16[128,4096]{1,0:T(8,128)(2,1)}, u32[]{:S(2)}, u32[]{:S(2)}) collective-permute-start(bf16[128,4096]{1,0:T(8,128)(2,1)} %get-tuple-element.75), channel_id=1, source_target_pairs={{2,0},{4,2},{6,4},{10,8},{12,10},{14,12},{18,16},{20,18},{22,20},{... | collective-permute-start | bytes 3145736 | tf_op jit(solution)/shard_map/ppermute | solution.py:309
  63.9 15.2 %collective-permute-start.12 = (bf16[1,1024,256]{2,1,0:T(8,128)(2,1)}, bf16[1,1024,256]{2,1,0:T(8,128)(2,1)}, u32[]{:S(2)}, u32[]{:S(2)}) collective-permute-start(bf16[1,1024,256]{2,1,0:T(8,128)(2,1)} %bitcast.5.refs_8_), channel_id=1, source_target_pairs={{0,16},{8,24},{16,0},{24,8},{1,17},{9,25},{17,1},{25,9},{2,18},{10... | collective-permute-start | bytes 1572872 | tf_op jit(solution)/shard_map/ppermute | solution.py:19
  65.7 13.4 %collective-permute-start.11 = (bf16[1,1024,256]{2,1,0:T(8,128)(2,1)}, bf16[1,1024,256]{2,1,0:T(8,128)(2,1)}, u32[]{:S(2)}, u32[]{:S(2)}) collective-permute-start(bf16[1,1024,256]{2,1,0:T(8,128)(2,1)} %bitcast.5.refs_8_), channel_id=1, source_target_pairs={{0,8},{8,0},{16,24},{24,16},{1,9},{9,1},{17,25},{25,17},{2,10},{10... | collective-permute-start | bytes 1572872 | tf_op jit(solution)/shard_map/ppermute | solution.py:19
  66.7 21.4 %collective-permute-start.3 = (bf16[1,1024,256]{2,1,0:T(8,128)(2,1)S(1)}, bf16[1,1024,256]{2,1,0:T(8,128)(2,1)S(1)}, u32[]{:S(2)}, u32[]{:S(2)}) collective-permute-start(bf16[1,1024,256]{2,1,0:T(8,128)(2,1)S(1)} %collective-permute-done.1.refs_1_), channel_id=1, source_target_pairs={{0,16},{8,24},{16,0},{24,8},{1,17},{9,25},{17,1},{25,9},{2,18},{10... | collective-permute-start | bytes 1572872 | tf_op jit(solution)/shard_map/ppermute | solution.py:19
  88.1 13.4 %collective-permute-start.9 = (bf16[1,1024,256]{2,1,0:T(8,128)(2,1)S(1)}, bf16[1,1024,256]{2,1,0:T(8,128)(2,1)S(1)}, u32[]{:S(2)}, u32[]{:S(2)}) collective-permute-start(bf16[1,1024,256]{2,1,0:T(8,128)(2,1)S(1)} %copy-done.8), channel_id=1, source_target_pairs={{0,8},{8,0},{16,24},{24,16},{1,9},{9,1},{17,25},{25,17},{2,10},{10... | collective-permute-start | bytes 1572872 | tf_op jit(solution)/shard_map/ppermute | solution.py:19
  89.7 23.5 %collective-permute-start.21 = (bf16[1024,256]{1,0:T(8,128)(2,1)S(1)}, bf16[1024,256]{1,0:T(8,128)(2,1)S(1)}, u32[]{:S(2)}, u32[]{:S(2)}) collective-permute-start(bf16[1024,256]{1,0:T(8,128)(2,1)S(1)} %get-tuple-element.84), channel_id=1, source_target_pairs={{0,6},{1,7},{2,4},{3,5},{4,2},{5,3},{6,0},{7,1},{8,14},{9,15},{10,... | collective-permute-start | bytes 1572872 | tf_op jit(solution)/shard_map/ppermute | solution.py:19
  101.5 15.1 %collective-permute-start.13 = (bf16[1,1024,256]{2,1,0:T(8,128)(2,1)}, bf16[1,1024,256]{2,1,0:T(8,128)(2,1)S(1)}, u32[]{:S(2)}, u32[]{:S(2)}) collective-permute-start(bf16[1,1024,256]{2,1,0:T(8,128)(2,1)} %collective-permute-done.11.refs_9_), channel_id=1, source_target_pairs={{0,16},{8,24},{16,0},{24,8},{1,17},{9,25},{17,1},{25,9},{2,18},{10... | collective-permute-start | bytes 1572872 | tf_op jit(solution)/shard_map/ppermute | solution.py:19
  102.9 21.2 %collective-permute-start.19 = (bf16[1,1024,256]{2,1,0:T(8,128)(2,1)S(1)}, bf16[1,1024,256]{2,1,0:T(8,128)(2,1)S(1)}, u32[]{:S(2)}, u32[]{:S(2)}) collective-permute-start(bf16[1,1024,256]{2,1,0:T(8,128)(2,1)S(1)} %bitcast.25), channel_id=1, source_target_pairs={{0,16},{8,24},{16,0},{24,8},{1,17},{9,25},{17,1},{25,9},{2,18},{10... | collective-permute-start | bytes 1572872 | tf_op jit(solution)/shard_map/ppermute | solution.py:19
  113.2 18.9 %collective-permute-start.22 = (bf16[1,1024,256]{2,1,0:T(8,128)(2,1)S(1)}, bf16[1,1024,256]{2,1,0:T(8,128)(2,1)S(1)}, u32[]{:S(2)}, u32[]{:S(2)}) collective-permute-start(bf16[1,1024,256]{2,1,0:T(8,128)(2,1)S(1)} %bitcast.34), channel_id=1, source_target_pairs={{0,8},{8,0},{16,24},{24,16},{1,9},{9,1},{17,25},{25,17},{2,10},{10... | collective-permute-start | bytes 1572872 | tf_op jit(solution)/shard_map/ppermute | solution.py:19
  124.1 13.5 %collective-permute-start.20 = (bf16[1,1024,256]{2,1,0:T(8,128)(2,1)S(1)}, bf16[1,1024,256]{2,1,0:T(8,128)(2,1)S(1)}, u32[]{:S(2)}, u32[]{:S(2)}) collective-permute-start(bf16[1,1024,256]{2,1,0:T(8,128)(2,1)S(1)} %collective-permute-done.19.refs_14_), channel_id=1, source_target_pairs={{0,8},{8,0},{16,24},{24,16},{1,9},{9,1},{17,25},{25,17},{2,10},{10... | collective-permute-start | bytes 1572872 | tf_op jit(solution)/shard_map/ppermute | solution.py:19
  126.4 18.7 %collective-permute-start.23 = (bf16[1,1024,256]{2,1,0:T(8,128)(2,1)S(1)}, bf16[1,1024,256]{2,1,0:T(8,128)(2,1)S(1)}, u32[]{:S(2)}, u32[]{:S(2)}) collective-permute-start(bf16[1,1024,256]{2,1,0:T(8,128)(2,1)S(1)} %bitcast.35), channel_id=1, source_target_pairs={{0,16},{8,24},{16,0},{24,8},{1,17},{9,25},{17,1},{25,9},{2,18},{10... | collective-permute-start | bytes 1572872 | tf_op jit(solution)/shard_map/ppermute | solution.py:19
  137.6 15.0 %collective-permute-start.24 = (bf16[1,1024,256]{2,1,0:T(8,128)(2,1)S(1)}, bf16[1,1024,256]{2,1,0:T(8,128)(2,1)S(1)}, u32[]{:S(2)}, u32[]{:S(2)}) collective-permute-start(bf16[1,1024,256]{2,1,0:T(8,128)(2,1)S(1)} %collective-permute-done.22.refs_17_), channel_id=1, source_target_pairs={{0,16},{8,24},{16,0},{24,8},{1,17},{9,25},{17,1},{25,9},{2,18},{10... | collective-permute-start | bytes 1572872 | tf_op jit(solution)/shard_map/ppermute | solution.py:19
  145.2 18.0 %collective-permute-start.37 = (bf16[3,384,256]{2,1,0:T(8,128)(2,1)S(1)}, bf16[3,384,256]{2,1,0:T(8,128)(2,1)S(1)}, u32[]{:S(2)}, u32[]{:S(2)}) collective-permute-start(bf16[3,384,256]{2,1,0:T(8,128)(2,1)S(1)} %pad_maximum_fusion.refs_20_), channel_id=1, source_target_pairs={{0,16},{8,24},{16,0},{24,8},{1,17},{9,25},{17,1},{25,9},{2,18},{10... | collective-permute-start | bytes 1769480 | tf_op jit(solution)/shard_map/ppermute | solution.py:19
  145.5 19.5 %collective-permute-start.34 = (bf16[3,384,256]{2,1,0:T(8,128)(2,1)S(1)}, bf16[3,384,256]{2,1,0:T(8,128)(2,1)S(1)}, u32[]{:S(2)}, u32[]{:S(2)}) collective-permute-start(bf16[3,384,256]{2,1,0:T(8,128)(2,1)S(1)} %pad_maximum_fusion.refs_20_), channel_id=1, source_target_pairs={{0,8},{8,0},{16,24},{24,16},{1,9},{9,1},{17,25},{25,17},{2,10},{10... | collective-permute-start | bytes 1769480 | tf_op jit(solution)/shard_map/ppermute | solution.py:19
  145.9 17.2 %collective-permute-start.26 = (bf16[320,256]{1,0:T(8,128)(2,1)S(1)}, bf16[320,256]{1,0:T(8,128)(2,1)S(1)}, u32[]{:S(2)}, u32[]{:S(2)}) collective-permute-start(bf16[320,256]{1,0:T(8,128)(2,1)S(1)} %get-tuple-element.92), channel_id=1, source_target_pairs={{0,2},{1,3},{2,0},{3,1},{4,6},{5,7},{6,4},{7,5},{8,10},{9,11},{10,... | collective-permute-start | bytes 491528 | tf_op jit(solution)/shard_map/ppermute | solution.py:19
  145.9 17.2 %collective-permute-start.29 = (bf16[320,256]{1,0:T(8,128)(2,1)S(1)}, bf16[320,256]{1,0:T(8,128)(2,1)S(1)}, u32[]{:S(2)}, u32[]{:S(2)}) collective-permute-start(bf16[320,256]{1,0:T(8,128)(2,1)S(1)} %get-tuple-element.98), channel_id=1, source_target_pairs={{0,4},{1,5},{2,6},{3,7},{4,0},{5,1},{6,2},{7,3},{8,12},{9,13},{10,... | collective-permute-start | bytes 491528 | tf_op jit(solution)/shard_map/ppermute | solution.py:19
  163.1 23.9 %collective-permute-start.40 = (bf16[3,384,256]{2,1,0:T(8,128)(2,1)S(1)}, bf16[3,384,256]{2,1,0:T(8,128)(2,1)S(1)}, u32[]{:S(2)}, u32[]{:S(2)}) collective-permute-start(bf16[3,384,256]{2,1,0:T(8,128)(2,1)S(1)} %collective-permute-done.37.refs_22_), channel_id=1, source_target_pairs={{0,8},{8,0},{16,24},{24,16},{1,9},{9,1},{17,25},{25,17},{2,10},{10... | collective-permute-start | bytes 1769480 | tf_op jit(solution)/shard_map/ppermute | solution.py:19
  163.2 19.3 %collective-permute-start.38 = (bf16[3,320,256]{2,1,0:T(8,128)(2,1)S(1)}, bf16[3,320,256]{2,1,0:T(8,128)(2,1)S(1)}, u32[]{:S(2)}, u32[]{:S(2)}) collective-permute-start(bf16[3,320,256]{2,1,0:T(8,128)(2,1)S(1)} %pad_maximum_fusion.2.refs_20_), channel_id=1, source_target_pairs={{0,16},{8,24},{16,0},{24,8},{1,17},{9,25},{17,1},{25,9},{2,18},{10... | collective-permute-start | bytes 1474568 | tf_op jit(solution)/shard_map/ppermute | solution.py:19
  165.1 21.9 %collective-permute-start.35 = (bf16[3,320,256]{2,1,0:T(8,128)(2,1)S(1)}, bf16[3,320,256]{2,1,0:T(8,128)(2,1)}, u32[]{:S(2)}, u32[]{:S(2)}) collective-permute-start(bf16[3,320,256]{2,1,0:T(8,128)(2,1)S(1)} %pad_maximum_fusion.2.refs_20_), channel_id=1, source_target_pairs={{0,8},{8,0},{16,24},{24,16},{1,9},{9,1},{17,25},{25,17},{2,10},{10... | collective-permute-start | bytes 1474568 | tf_op jit(solution)/shard_map/ppermute | solution.py:19
  182.5 22.8 %collective-permute-start.39 = (bf16[3,320,256]{2,1,0:T(8,128)(2,1)}, bf16[3,320,256]{2,1,0:T(8,128)(2,1)}, u32[]{:S(2)}, u32[]{:S(2)}) collective-permute-start(bf16[3,320,256]{2,1,0:T(8,128)(2,1)} %pad_maximum_fusion.1.refs_20_), channel_id=1, source_target_pairs={{0,16},{8,24},{16,0},{24,8},{1,17},{9,25},{17,1},{25,9},{2,18},{10... | collective-permute-start | bytes 1474568 | tf_op jit(solution)/shard_map/ppermute | solution.py:19
  187.9 17.5 %collective-permute-start.41 = (bf16[3,320,256]{2,1,0:T(8,128)(2,1)}, bf16[3,320,256]{2,1,0:T(8,128)(2,1)}, u32[]{:S(2)}, u32[]{:S(2)}) collective-permute-start(bf16[3,320,256]{2,1,0:T(8,128)(2,1)} %collective-permute-done.35.refs_21_), channel_id=1, source_target_pairs={{0,16},{8,24},{16,0},{24,8},{1,17},{9,25},{17,1},{25,9},{2,18},{10... | collective-permute-start | bytes 1474568 | tf_op jit(solution)/shard_map/ppermute | solution.py:19
  189.3 31.3 %collective-permute-start.36 = (bf16[3,320,256]{2,1,0:T(8,128)(2,1)}, bf16[3,320,256]{2,1,0:T(8,128)(2,1)S(1)}, u32[]{:S(2)}, u32[]{:S(2)}) collective-permute-start(bf16[3,320,256]{2,1,0:T(8,128)(2,1)} %pad_maximum_fusion.1.refs_20_), channel_id=1, source_target_pairs={{0,8},{8,0},{16,24},{24,16},{1,9},{9,1},{17,25},{25,17},{2,10},{10... | collective-permute-start | bytes 1474568 | tf_op jit(solution)/shard_map/ppermute | solution.py:19
  205.4 15.2 %collective-permute-start.42 = (bf16[3,320,256]{2,1,0:T(8,128)(2,1)}, bf16[3,320,256]{2,1,0:T(8,128)(2,1)S(1)}, u32[]{:S(2)}, u32[]{:S(2)}) collective-permute-start(bf16[3,320,256]{2,1,0:T(8,128)(2,1)} %collective-permute-done.39.refs_22_), channel_id=1, source_target_pairs={{0,8},{8,0},{16,24},{24,16},{1,9},{9,1},{17,25},{25,17},{2,10},{10... | collective-permute-start | bytes 1474568 | tf_op jit(solution)/shard_map/ppermute | solution.py:19
  (39 other events, 1076.2 us)

commit v3 on v2

--- a/solution.py
+++ b/solution.py
@@ -10,7 +10,7 @@
 
 BOUNDS = (0, 6, 11, 16)
 ROW_STEPS = 4
-PAIRS = 2
+PAIRS = 4
 FOLD_VMEM = 28 * 1024 * 1024
 CORRELATE_VMEM = 60 * 1024 * 1024
 
@@ -39,7 +39,7 @@
 
 
 def spectra_kernel(late, cuts, scale, core_ref, weights_ref, table_ref, *refs):
-    sources = 6 if late else 2
+    sources = 4 if late else 2
     inputs, outs = refs[:sources], refs[sources:-4]
     samples, folded, spread, sems = refs[-4:]
     core = core_ref[0]
@@ -58,13 +58,12 @@
             sems.at[which, step],
         )
 
-    def halo_copy(refs, step, which):
+    def halo_copy(ref, step):
         rows = pl.ds(step * step_rows, step_rows)
-        start = slab + which * refs[0].shape[1]
         return pltpu.make_async_copy(
-            refs[which].at[pl.ds(step * step_rows % half_rows, step_rows), :],
-            samples.at[rows, pl.ds(start, refs[which].shape[1])],
-            sems.at[1 + which, step],
+            ref.at[pl.ds(step * step_rows % half_rows, step_rows), :],
+            samples.at[rows, pl.ds(slab, tail)],
+            sems.at[1, step],
         )
 
     def start_all(first, second):
@@ -89,19 +88,16 @@
 
             @pl.when(core == half)
             def _():
-                halo_copy(inputs[2:4], step, 0).start()
-                halo_copy(inputs[2:4], step, 1).start()
+                halo_copy(inputs[2], step).start()
 
             @pl.when(core != half)
             def _():
-                halo_copy(inputs[4:6], step, 0).start()
-                halo_copy(inputs[4:6], step, 1).start()
+                halo_copy(inputs[3], step).start()
 
     for step in range(ROW_STEPS):
         slab_copy(own, step, slab, 0, 0).wait()
         if late:
-            halo_copy(inputs[2:4], step, 0).wait()
-            halo_copy(inputs[2:4], step, 1).wait()
+            halo_copy(inputs[2], step).wait()
         else:
             slab_copy(own, step, tail, slab, 1).wait()
 
@@ -164,7 +160,7 @@
             pltpu.VMEM((count, (frames + depth - 1) * width), jnp.bfloat16),
             pltpu.VMEM((frames, count, width), jnp.bfloat16),
             pltpu.VMEM((count // 128, channels * frames, 128), jnp.float32),
-            pltpu.SemaphoreType.DMA((3, ROW_STEPS)),
+            pltpu.SemaphoreType.DMA((2, ROW_STEPS)),
         ],
         compiler_params=pltpu.CompilerParams(vmem_limit_bytes=FOLD_VMEM),
         cost_estimate=pl.CostEstimate(flops=1, bytes_accessed=1, transcendentals=0),
@@ -198,8 +194,8 @@
 
     depth = len(pieces) * 16
     places = lax.broadcasted_iota(jnp.int32, (count, depth), 1)
-    even = jnp.where(places % 16 < 8, 1.0, 0.0).astype(jnp.bfloat16)
-    odd = jnp.where(places % 16 < 8, 0.0, 1.0).astype(jnp.bfloat16)
+    even = jnp.where(places % 16 < 8, scale, 0.0).astype(jnp.bfloat16)
+    odd = jnp.where(places % 16 < 8, 0.0, scale).astype(jnp.bfloat16)
     for pair in range(PAIRS):
         rows = slice(pair * 16, pair * 16 + 16)
 
@@ -217,7 +213,7 @@
         turned = stack(0).T
         left = jnp.concatenate([turned * even, turned * odd], axis=0)
         for member in range(groups):
-            summed = scale * lax.dot_general(
+            summed = lax.dot_general(
                 left, stack(member), (((1,), (0,)), ((), ())), preferred_element_type=jnp.float32
             )
             columns = pl.ds(pl.multiple_of((group ^ member) * count, 128), count)
@@ -302,21 +298,9 @@
     other = swap(voltages, "chan", 1)
     route = [[(2 * p + 2, 2 * p + k) for p in range(parts - 1)] for k in (0, 1)]
     tail = (depth - 1) * width
-    split = width * ((depth - 1) // 2)
-
-    def ahead_of(first, stop, *events):
-        return [
-            lax.ppermute(
-                after(voltages[k * half : k * half + half, first:stop], *events), "chan", route[k]
-            )
-            for k in (0, 1)
-        ]
-
-    def swapped(pair):
-        mine = jnp.where(core == 0, pair[0], pair[1])
-        return mine, swap(mine, "chan", 1)
-
-    ahead = ahead_of(0, split)
+    sliced = [voltages[k * half : k * half + half, :tail] for k in (0, 1)]
+    ahead = [lax.ppermute(sliced[k], "chan", route[k]) for k in (0, 1)]
+    other = after(other, *sliced)
 
     owned = (place // 2) ^ jnp.arange(parts, dtype=jnp.int32)
     table = cosine_rows((owned * 2 + core) * channels, channels, width)
@@ -327,27 +311,26 @@
     cuts = [(part * channels, channels) for part in range(parts)]
     early = spectra_blocks(False, cuts, at_core, weights, table, [voltages, other])
     own_early = joined(early[0][None], 0)
-    near = swap(after(early[1], *ahead), "chan", 2)
-    middle = swap(after(early[2], *ahead), "chan", 4)
+    near = swap(early[1], "chan", 2)
     near_joined = joined(near[None], 1, own_early)
-    middle_joined = joined(middle[None], 0, near_joined)
-    rest = ahead_of(split, tail, near, middle, *own_early[1:3])
-    far = [swap(after(early[part], *rest), "chan", 2 * part) for part in range(3, parts)]
-    halo, other_halo = swapped(ahead)
-    rest = lax.optimization_barrier((*rest, *middle_joined[1:3]))[:2]
-    halo_rest, other_rest = swapped(rest)
-    sources = [voltages, other, halo, halo_rest, other_halo, other_rest]
-    bounds = [round(channels * bound / 64) * 4 for bound in BOUNDS]
+    middle = swap(after(early[2], near), "chan", 4)
+    far = [swap(after(early[part], middle), "chan", 2 * part) for part in range(3, parts)]
+
+    ahead = lax.optimization_barrier((ahead[0], ahead[1], near, *own_early[1:]))
+    halo = jnp.where(core == 0, ahead[0], ahead[1])
+    other_halo = swap(halo, "chan", 1)
+    bounds = [round(channels * bound / (32 * PAIRS)) * 2 * PAIRS for bound in BOUNDS]
     blocks = list(zip(bounds[:-1], bounds[1:]))
     cuts = [(0, channels)] + [
         (part * channels + first, stop - first)
         for first, stop in blocks
         for part in range(1, parts)
     ]
-    late = spectra_blocks(True, cuts, at_core, weights, table, sources)
-    own_late = joined(late[0][None], 1, middle_joined)
-    far_joined = joined(jnp.stack(far), 0, own_late)
-    wide = [own_early, near_joined, middle_joined, own_late, far_joined]
+    late = spectra_blocks(True, cuts, at_core, weights, table, [voltages, other, halo, other_halo])
+    own_late = joined(late[0][None], 0, near_joined)
+    middle_joined = joined(middle[None], 1, own_late)
+    far_joined = joined(jnp.stack(far), 0, middle_joined)
+    wide = [own_early, near_joined, own_late, middle_joined, far_joined]
     landed, narrow, results = [near, middle] + far, [far_joined], [None]
     for chunk, (first, stop) in enumerate(blocks):
         skipped = chunk * (parts - 1)

time: 239 us -> 229 us (0.958)
  starting transfers between devices: 52.2 us -> 42.8 us
  waiting for transfers between devices: 106 us -> 115 us
  Pallas kernels: 61.3 us -> 55.4 us
    ppermute x4 -> x2, waiting for transfers between devices: 0.35 us -> 10.7 us  [on_device(): ahead = [lax.ppermute(sliced[k], 'chan', route[k]) for k in (0, 1)]]
    pallas_call x3, Pallas kernels: 42.4 us -> 36.7 us  [correlate(): pl.pallas_call(functools.partial(correlate_kernel, 1.0 / frames, groups,...]
    ppermute x4 -> x2, starting transfers between devices: 11.4 us -> 5.71 us  [on_device(): ahead = [lax.ppermute(sliced[k], 'chan', route[k]) for k in (0, 1)]]
    ppermute x39 -> x38, starting transfers between devices: 40.8 us -> 37.1 us  [swap(): lax.ppermute(block, axis, [(i, i ^ bit) for i in range(lax.axis_size(axis...]
    ppermute x39 -> x38, waiting for transfers between devices: 106 us -> 104 us  [swap(): lax.ppermute(block, axis, [(i, i ^ bit) for i in range(lax.axis_size(axis...]
    unnamed x56 -> x54, local copies, waits for them, and re-layouts: 5.83 us -> 4.62 us
  transfers between devices with their start and end apart: 43 -> 40, of which waited for: 17 -> 19; matrix products, arithmetic and copies ran while one was open for 4% -> 3% of each run, Pallas kernels for 20% -> 19%
where the time goes in v3:
time: 229 us; the launch traced here: 227 us
  waiting for transfers between devices  115 us (50%)
  Pallas kernels  55.4 us (24%)
  starting transfers between devices  42.8 us (19%)
  local copies, waits for them, and re-layouts  8.88 us (4%)
  other arithmetic  4.06 us (2%)
    ppermute x38, waiting for transfers between devices, swap(): lax.ppermute(block, axis, [(i, i ^ bit) for i in range(lax.axis_size(axis...  104 us
    ppermute x38, starting transfers between devices, swap(): lax.ppermute(block, axis, [(i, i ^ bit) for i in range(lax.axis_size(axis...  37.1 us
    pallas_call x3, Pallas kernels, correlate(): pl.pallas_call(functools.partial(correlate_kernel, 1.0 / frames, groups,...  36.7 us
    pallas_call x2, Pallas kernels, spectra_blocks(): pl.pallas_call(functools.partial(spectra_kernel, late, cuts, math.sqrt(2....  18.7 us
    ppermute x2, waiting for transfers between devices, on_device(): ahead = [lax.ppermute(sliced[k], 'chan', route[k]) for k in (0, 1)]  10.7 us
    ppermute x2, starting transfers between devices, on_device(): ahead = [lax.ppermute(sliced[k], 'chan', route[k]) for k in (0, 1)]  5.71 us
    unnamed x54, local copies, waits for them, and re-layouts  4.62 us
  transfers between devices with their start and end apart: 40, of which 19 were waited for; matrix products, arithmetic and copies ran while one was open for 3% of the time, Pallas kernels for 19%

profile of v3, /device:TPU:16, one launch (start us, length us, event | category | flops | bytes accessed | tf_op | source)
XLA Modules:
  0.0 226.6 jit_solution(5157511242084852376)
XLA Ops:
  0.0 4.2 %fusion.10 = (bf16[128,7168]{1,0:T(8,128)(2,1)}, bf16[128,7168]{1,0:T(8,128)(2,1)}) fusion(bf16[256,8192]{1,0:T(8,128)(2,1)} %refs_0_.3), kind=kLoop, calls=%fused_computation.33 | loop fusion | bytes 7340032 | tf_op jit(solution)/shard_map/slice | solution.py:301
  4.2 2.3 %collective-permute-start.8 = (bf16[128,7168]{1,0:T(8,128)(2,1)}, bf16[128,7168]{1,0:T(8,128)(2,1)}, u32[]{:S(2)}, u32[]{:S(2)}) collective-permute-start(bf16[128,7168]{1,0:T(8,128)(2,1)} %get-tuple-element.112), channel_id=1, source_target_pairs={{2,0},{4,2},{6,4},{10,8},{12,10},{14,12},{18,16},{20,18},{22,20},{... | collective-permute-start | bytes 5505032 | tf_op jit(solution)/shard_map/ppermute | solution.py:302
  6.5 3.4 %collective-permute-start.9 = (bf16[128,7168]{1,0:T(8,128)(2,1)}, bf16[128,7168]{1,0:T(8,128)(2,1)}, u32[]{:S(2)}, u32[]{:S(2)}) collective-permute-start(bf16[128,7168]{1,0:T(8,128)(2,1)} %get-tuple-element.111), channel_id=1, source_target_pairs={{2,1},{4,3},{6,5},{10,9},{12,11},{14,13},{18,17},{20,19},{22,21},{... | collective-permute-start | bytes 5505032 | tf_op jit(solution)/shard_map/ppermute | solution.py:302
  11.4 2.2 copy-done
  13.6 9.4 %fold_transform.2 = (bf16[1024,256]{1,0:T(8,128)(2,1)S(1)}, bf16[1024,256]{1,0:T(8,128)(2,1)S(1)}, bf16[1024,256]{1,0:T(8,128)(2,1)S(1)}, bf16[1024,256]{1,0:T(8,128)(2,1)S(1)}) custom-call(s32[1]{0:T(128)} %bitcast.1.core_ref, f32[8,1024]{1,0:T(8,128)S(1)} %broadcast_multiply_fusion.weights_ref, bf16[512,1024]{1,0:T(8,128)(2,1)S(1)} %bitcast.17, ...), custom_call_target="tpu_custom_call" | custom-call | flops 1 | bytes 1 | tf_op jit(solution)/shard_map/fold_transform/pallas_call | solution.py:153
  23.0 1.5 collective-permute-start.1
  24.6 1.5 collective-permute-start.2
  26.1 2.1 collective-permute-start.4
  28.2 6.9 %collective-permute-done.1.refs_1_ = bf16[1,1024,256]{2,1,0:T(8,128)(2,1)} collective-permute-done((bf16[1,1024,256]{2,1,0:T(8,128)(2,1)S(1)}, bf16[1,1024,256]{2,1,0:T(8,128)(2,1)}, u32[]{:S(2)}, u32[]{:S(2)}) %collective-permute-start.1) | collective-permute-done | bytes 524320 | tf_op jit(solution)/shard_map/ppermute | solution.py:19
  36.6 10.7 %collective-permute-done.9 = bf16[128,7168]{1,0:T(8,128)(2,1)} collective-permute-done((bf16[128,7168]{1,0:T(8,128)(2,1)}, bf16[128,7168]{1,0:T(8,128)(2,1)}, u32[]{:S(2)}, u32[]{:S(2)}) %collective-permute-start.9) | collective-permute-done | bytes 1835040 | tf_op jit(solution)/shard_map/ppermute | solution.py:302
  47.2 13.3 %collective-permute-done.4 = bf16[1024,256]{1,0:T(8,128)(2,1)} collective-permute-done((bf16[1024,256]{1,0:T(8,128)(2,1)S(1)}, bf16[1024,256]{1,0:T(8,128)(2,1)}, u32[]{:S(2)}, u32[]{:S(2)}) %collective-permute-start.4) | collective-permute-done | bytes 524320 | tf_op jit(solution)/shard_map/ppermute | solution.py:19
  60.5 1.7 broadcast_select_fusion.refs_2_
  62.3 1.6 collective-permute-start.5
  66.1 9.3 %fold_transform.3 = (bf16[1024,256]{1,0:T(8,128)(2,1)S(1)}, bf16[384,256]{1,0:T(8,128)(2,1)S(1)}, bf16[384,256]{1,0:T(8,128)(2,1)S(1)}, bf16[384,256]{1,0:T(8,12...) custom-call(s32[1]{0:T(128)} %bitcast.1.core_ref, ...), custom_call_target="tpu_custom_call" | custom-call | flops 1 | bytes 1 | tf_op jit(solution)/shard_map/fold_transform/pallas_call | solution.py:153
  80.4 6.7 %collective-permute-done.14 = bf16[1024,256]{1,0:T(8,128)(2,1)S(1)} collective-permute-done((bf16[1024,256]{1,0:T(8,128)(2,1)S(1)}, bf16[1024,256]{1,0:T(8,128)(2,1)S(1)}, u32[]{:S(2)}, u32[]{:S(2)}) %collective-permute-start.14) | collective-permute-done | bytes 524320 | tf_op jit(solution)/shard_map/ppermute | solution.py:19
  87.0 1.7 collective-permute-start.18
  88.7 2.9 %collective-permute-done.11.refs_9_ = bf16[1,1024,256]{2,1,0:T(8,128)(2,1)S(1)} collective-permute-done((bf16[1,1024,256]{2,1,0:T(8,128)(2,1)S(1)}, bf16[1,1024,256]{2,1,0:T(8,128)(2,1)S(1)}, u32[]{:S(2)}, u32[]{:S(2)}) %collective-permute-start.11) | collective-permute-done | bytes 524320 | tf_op jit(solution)/shard_map/ppermute | solution.py:19
  94.7 8.2 %collective-permute-done.7.refs_7_ = bf16[1,1024,256]{2,1,0:T(8,128)(2,1)S(1)} collective-permute-done((bf16[1,1024,256]{2,1,0:T(8,128)(2,1)S(1)}, bf16[1,1024,256]{2,1,0:T(8,128)(2,1)S(1)}, u32[]{:S(2)}, u32[]{:S(2)}) %collective-permute-start.7) | collective-permute-done | bytes 524320 | tf_op jit(solution)/shard_map/ppermute | solution.py:19
  104.4 7.7 %collective-permute-done.18 = bf16[1024,256]{1,0:T(8,128)(2,1)S(1)} collective-permute-done((bf16[1024,256]{1,0:T(8,128)(2,1)S(1)}, bf16[1024,256]{1,0:T(8,128)(2,1)S(1)}, u32[]{:S(2)}, u32[]{:S(2)}) %collective-permute-start.18) | collective-permute-done | bytes 524320 | tf_op jit(solution)/shard_map/ppermute | solution.py:19
  117.4 1.5 collective-permute-start.22
  119.1 8.6 %collective-permute-done.19.refs_17_ = bf16[1,1024,256]{2,1,0:T(8,128)(2,1)S(1)} collective-permute-done((bf16[1,1024,256]{2,1,0:T(8,128)(2,1)S(1)}, bf16[1,1024,256]{2,1,0:T(8,128)(2,1)S(1)}, u32[]{:S(2)}, u32[]{:S(2)}) %collective-permute-start.19) | collective-permute-done | bytes 524320 | tf_op jit(solution)/shard_map/ppermute | solution.py:19
  127.8 8.9 %collective-permute-done.17.refs_15_ = bf16[1,1024,256]{2,1,0:T(8,128)(2,1)S(1)} collective-permute-done((bf16[1,1024,256]{2,1,0:T(8,128)(2,1)S(1)}, bf16[1,1024,256]{2,1,0:T(8,128)(2,1)S(1)}, u32[]{:S(2)}, u32[]{:S(2)}) %collective-permute-start.17) | collective-permute-done | bytes 524320 | tf_op jit(solution)/shard_map/ppermute | solution.py:19
  140.7 10.8 %collective-permute-done.21.refs_19_ = bf16[1,1024,256]{2,1,0:T(8,128)(2,1)S(1)} collective-permute-done((bf16[1,1024,256]{2,1,0:T(8,128)(2,1)S(1)}, bf16[1,1024,256]{2,1,0:T(8,128)(2,1)S(1)}, u32[]{:S(2)}, u32[]{:S(2)}) %collective-permute-start.21) | collective-permute-done | bytes 524320 | tf_op jit(solution)/shard_map/ppermute | solution.py:19
  151.5 9.4 %collective-permute-done.34.refs_22_ = bf16[3,384,256]{2,1,0:T(8,128)(2,1)S(1)} collective-permute-done((bf16[3,384,256]{2,1,0:T(8,128)(2,1)S(1)}, bf16[3,384,256]{2,1,0:T(8,128)(2,1)S(1)}, u32[]{:S(2)}, u32[]{:S(2)}) %collective-permute-start.34) | collective-permute-done | bytes 589856 | tf_op jit(solution)/shard_map/ppermute | solution.py:19
  162.5 1.6 collective-permute-start.35
  165.0 5.6 %collective-permute-done.24 = bf16[320,256]{1,0:T(8,128)(2,1)S(1)} collective-permute-done((bf16[320,256]{1,0:T(8,128)(2,1)S(1)}, bf16[320,256]{1,0:T(8,128)(2,1)S(1)}, u32[]{:S(2)}, u32[]{:S(2)}) %collective-permute-start.24) | collective-permute-done | bytes 163872 | tf_op jit(solution)/shard_map/ppermute | solution.py:19
  170.6 2.3 collective-permute-done.27
  172.9 3.7 %collective-permute-done.30 = bf16[320,256]{1,0:T(8,128)(2,1)S(1)} collective-permute-done((bf16[320,256]{1,0:T(8,128)(2,1)S(1)}, bf16[320,256]{1,0:T(8,128)(2,1)S(1)}, u32[]{:S(2)}, u32[]{:S(2)}) %collective-permute-start.30) | collective-permute-done | bytes 163872 | tf_op jit(solution)/shard_map/ppermute | solution.py:19
  178.0 5.7 %collective-permute-done.32.refs_21_ = bf16[3,320,256]{2,1,0:T(8,128)(2,1)} collective-permute-done((bf16[3,320,256]{2,1,0:T(8,128)(2,1)S(1)}, bf16[3,320,256]{2,1,0:T(8,128)(2,1)}, u32[]{:S(2)}, u32[]{:S(2)}) %collective-permute-start.32) | collective-permute-done | bytes 491552 | tf_op jit(solution)/shard_map/ppermute | solution.py:19
  187.7 13.4 %correlate.3.refs_24_ = bf16[128,256,1024]{2,1,0:T(8,128)(2,1)} custom-call(s32[1]{0:T(128)} %bitcast.group_ref, bf16[1,1024,256]{2,1,0:T(8,128)(2,1)} %bitcast.21, bf16[1,1024,256]{2,1,0:T(8,128)(2,1)} %collective-permute-done.1.refs_1_, bf16[1,1024,256]{2,1,0:T(8,128)(2,1)} %collective-permute-done.2.refs_2_, ...), custom_call_target="tpu_custom_call" | custom-call | flops 1 | bytes 1 | tf_op jit(solution)/shard_map/correlate/pallas_call | solution.py:252
  201.6 11.6 %correlate.4.refs_24_ = bf16[128,256,1024]{2,1,0:T(8,128)(2,1)} custom-call(s32[1]{0:T(128)} %bitcast.group_ref, bf16[1,1024,256]{2,1,0:T(8,128)(2,1)} %bitcast.22, bf16[1,1024,256]{2,1,0:T(8,128)(2,1)} %collective-permute-done.1.refs_1_, bf16[1,1024,256]{2,1,0:T(8,128)(2,1)} %collective-permute-done.2.refs_2_, ...), custom_call_target="tpu_custom_call", output_to_operand_aliasing={{}: (25, {})} | custom-call | flops 1 | bytes 1 | tf_op jit(solution)/shard_map/correlate/pallas_call | solution.py:252
  214.8 11.6 %correlate.5 = bf16[128,256,1024]{2,1,0:T(8,128)(2,1)} custom-call(s32[1]{0:T(128)} %bitcast.group_ref, bf16[1,1024,256]{2,1,0:T(8,128)(2,1)} %bitcast.23, bf16[1,1024,256]{2,1,0:T(8,128)(2,1)} %collective-permute-done.1.refs_1_, bf16[1,1024,256]{2,1,0:T(8,128)(2,1)} %collective-permute-done.2.refs_2_, ...), custom_call_target="tpu_custom_call", output_to_operand_aliasing={{}: (25, {})} | custom-call | flops 1 | bytes 1 | tf_op jit(solution)/shard_map/correlate/pallas_call | solution.py:252
  (122 shorter events, 34.1 us)
Async XLA Ops:
  4.2 32.4 %collective-permute-start.8 = (bf16[128,7168]{1,0:T(8,128)(2,1)}, bf16[128,7168]{1,0:T(8,128)(2,1)}, u32[]{:S(2)}, u32[]{:S(2)}) collective-permute-start(bf16[128,7168]{1,0:T(8,128)(2,1)} %get-tuple-element.112), channel_id=1, source_target_pairs={{2,0},{4,2},{6,4},{10,8},{12,10},{14,12},{18,16},{20,18},{22,20},{... | collective-permute-start | bytes 5505032 | tf_op jit(solution)/shard_map/ppermute | solution.py:302
  6.5 40.7 %collective-permute-start.9 = (bf16[128,7168]{1,0:T(8,128)(2,1)}, bf16[128,7168]{1,0:T(8,128)(2,1)}, u32[]{:S(2)}, u32[]{:S(2)}) collective-permute-start(bf16[128,7168]{1,0:T(8,128)(2,1)} %get-tuple-element.111), channel_id=1, source_target_pairs={{2,1},{4,3},{6,5},{10,9},{12,11},{14,13},{18,17},{20,19},{22,21},{... | collective-permute-start | bytes 5505032 | tf_op jit(solution)/shard_map/ppermute | solution.py:302
  24.6 22.7 %collective-permute-start.2 = (bf16[1,1024,256]{2,1,0:T(8,128)(2,1)S(1)}, bf16[1,1024,256]{2,1,0:T(8,128)(2,1)}, u32[]{:S(2)}, u32[]{:S(2)}) collective-permute-start(bf16[1,1024,256]{2,1,0:T(8,128)(2,1)S(1)} %bitcast.20), channel_id=1, source_target_pairs={{0,16},{8,24},{16,0},{24,8},{1,17},{9,25},{17,1},{25,9},{2,18},{10... | collective-permute-start | bytes 1572872 | tf_op jit(solution)/shard_map/ppermute | solution.py:19
  26.1 34.4 %collective-permute-start.4 = (bf16[1024,256]{1,0:T(8,128)(2,1)S(1)}, bf16[1024,256]{1,0:T(8,128)(2,1)}, u32[]{:S(2)}, u32[]{:S(2)}) collective-permute-start(bf16[1024,256]{1,0:T(8,128)(2,1)S(1)} %get-tuple-element.64), channel_id=1, source_target_pairs={{0,2},{1,3},{2,0},{3,1},{4,6},{5,7},{6,4},{7,5},{8,10},{9,11},{10,... | collective-permute-start | bytes 1572872 | tf_op jit(solution)/shard_map/ppermute | solution.py:19
  35.1 25.4 %collective-permute-start.3 = (bf16[1,1024,256]{2,1,0:T(8,128)(2,1)}, bf16[1,1024,256]{2,1,0:T(8,128)(2,1)}, u32[]{:S(2)}, u32[]{:S(2)}) collective-permute-start(bf16[1,1024,256]{2,1,0:T(8,128)(2,1)} %collective-permute-done.1.refs_1_), channel_id=1, source_target_pairs={{0,16},{8,24},{16,0},{24,8},{1,17},{9,25},{17,1},{25,9},{2,18},{10... | collective-permute-start | bytes 1572872 | tf_op jit(solution)/shard_map/ppermute | solution.py:19
  62.3 14.6 %collective-permute-start.5 = (bf16[1,1024,256]{2,1,0:T(8,128)(2,1)}, bf16[1,1024,256]{2,1,0:T(8,128)(2,1)S(1)}, u32[]{:S(2)}, u32[]{:S(2)}) collective-permute-start(bf16[1,1024,256]{2,1,0:T(8,128)(2,1)} %bitcast.4.refs_4_), channel_id=1, source_target_pairs={{0,8},{8,0},{16,24},{24,16},{1,9},{9,1},{17,25},{25,17},{2,10},{10... | collective-permute-start | bytes 1572872 | tf_op jit(solution)/shard_map/ppermute | solution.py:19
  63.8 14.5 %collective-permute-start.6 = (bf16[1,1024,256]{2,1,0:T(8,128)(2,1)}, bf16[1,1024,256]{2,1,0:T(8,128)(2,1)S(1)}, u32[]{:S(2)}, u32[]{:S(2)}) collective-permute-start(bf16[1,1024,256]{2,1,0:T(8,128)(2,1)} %bitcast.4.refs_4_), channel_id=1, source_target_pairs={{0,16},{8,24},{16,0},{24,8},{1,17},{9,25},{17,1},{25,9},{2,18},{10... | collective-permute-start | bytes 1572872 | tf_op jit(solution)/shard_map/ppermute | solution.py:19
  65.4 21.7 %collective-permute-start.14 = (bf16[1024,256]{1,0:T(8,128)(2,1)S(1)}, bf16[1024,256]{1,0:T(8,128)(2,1)S(1)}, u32[]{:S(2)}, u32[]{:S(2)}) collective-permute-start(bf16[1024,256]{1,0:T(8,128)(2,1)S(1)} %get-tuple-element.75), channel_id=1, source_target_pairs={{0,4},{1,5},{2,6},{3,7},{4,0},{5,1},{6,2},{7,3},{8,12},{9,13},{10,... | collective-permute-start | bytes 1572872 | tf_op jit(solution)/shard_map/ppermute | solution.py:19
  76.8 14.8 %collective-permute-start.11 = (bf16[1,1024,256]{2,1,0:T(8,128)(2,1)S(1)}, bf16[1,1024,256]{2,1,0:T(8,128)(2,1)S(1)}, u32[]{:S(2)}, u32[]{:S(2)}) collective-permute-start(bf16[1,1024,256]{2,1,0:T(8,128)(2,1)S(1)} %bitcast.24), channel_id=1, source_target_pairs={{0,8},{8,0},{16,24},{24,16},{1,9},{9,1},{17,25},{25,17},{2,10},{10... | collective-permute-start | bytes 1572872 | tf_op jit(solution)/shard_map/ppermute | solution.py:19
  78.3 14.8 %collective-permute-start.12 = (bf16[1,1024,256]{2,1,0:T(8,128)(2,1)S(1)}, bf16[1,1024,256]{2,1,0:T(8,128)(2,1)S(1)}, u32[]{:S(2)}, u32[]{:S(2)}) collective-permute-start(bf16[1,1024,256]{2,1,0:T(8,128)(2,1)S(1)} %bitcast.25), channel_id=1, source_target_pairs={{0,16},{8,24},{16,0},{24,8},{1,17},{9,25},{17,1},{25,9},{2,18},{10... | collective-permute-start | bytes 1572872 | tf_op jit(solution)/shard_map/ppermute | solution.py:19
  79.9 23.1 %collective-permute-start.7 = (bf16[1,1024,256]{2,1,0:T(8,128)(2,1)S(1)}, bf16[1,1024,256]{2,1,0:T(8,128)(2,1)S(1)}, u32[]{:S(2)}, u32[]{:S(2)}) collective-permute-start(bf16[1,1024,256]{2,1,0:T(8,128)(2,1)S(1)} %collective-permute-done.6.refs_6_), channel_id=1, source_target_pairs={{0,8},{8,0},{16,24},{24,16},{1,9},{9,1},{17,25},{25,17},{2,10},{10... | collective-permute-start | bytes 1572872 | tf_op jit(solution)/shard_map/ppermute | solution.py:19
  87.0 25.1 %collective-permute-start.18 = (bf16[1024,256]{1,0:T(8,128)(2,1)S(1)}, bf16[1024,256]{1,0:T(8,128)(2,1)S(1)}, u32[]{:S(2)}, u32[]{:S(2)}) collective-permute-start(bf16[1024,256]{1,0:T(8,128)(2,1)S(1)} %get-tuple-element.80), channel_id=1, source_target_pairs={{0,6},{1,7},{2,4},{3,5},{4,2},{5,3},{6,0},{7,1},{8,14},{9,15},{10,... | collective-permute-start | bytes 1572872 | tf_op jit(solution)/shard_map/ppermute | solution.py:19
  91.7 21.1 %collective-permute-start.15 = (bf16[1,1024,256]{2,1,0:T(8,128)(2,1)S(1)}, bf16[1,1024,256]{2,1,0:T(8,128)(2,1)S(1)}, u32[]{:S(2)}, u32[]{:S(2)}) collective-permute-start(bf16[1,1024,256]{2,1,0:T(8,128)(2,1)S(1)} %bitcast.29), channel_id=1, source_target_pairs={{0,8},{8,0},{16,24},{24,16},{1,9},{9,1},{17,25},{25,17},{2,10},{10... | collective-permute-start | bytes 1572872 | tf_op jit(solution)/shard_map/ppermute | solution.py:19
  93.2 21.1 %collective-permute-start.16 = (bf16[1,1024,256]{2,1,0:T(8,128)(2,1)S(1)}, bf16[1,1024,256]{2,1,0:T(8,128)(2,1)S(1)}, u32[]{:S(2)}, u32[]{:S(2)}) collective-permute-start(bf16[1,1024,256]{2,1,0:T(8,128)(2,1)S(1)} %bitcast.30), channel_id=1, source_target_pairs={{0,16},{8,24},{16,0},{24,8},{1,17},{9,25},{17,1},{25,9},{2,18},{10... | collective-permute-start | bytes 1572872 | tf_op jit(solution)/shard_map/ppermute | solution.py:19
  102.9 12.5 %collective-permute-start.13 = (bf16[1,1024,256]{2,1,0:T(8,128)(2,1)S(1)}, bf16[1,1024,256]{2,1,0:T(8,128)(2,1)S(1)}, u32[]{:S(2)}, u32[]{:S(2)}) collective-permute-start(bf16[1,1024,256]{2,1,0:T(8,128)(2,1)S(1)} %collective-permute-done.11.refs_9_), channel_id=1, source_target_pairs={{0,16},{8,24},{16,0},{24,8},{1,17},{9,25},{17,1},{25,9},{2,18},{10... | collective-permute-start | bytes 1572872 | tf_op jit(solution)/shard_map/ppermute | solution.py:19
  112.8 14.9 %collective-permute-start.19 = (bf16[1,1024,256]{2,1,0:T(8,128)(2,1)S(1)}, bf16[1,1024,256]{2,1,0:T(8,128)(2,1)S(1)}, u32[]{:S(2)}, u32[]{:S(2)}) collective-permute-start(bf16[1,1024,256]{2,1,0:T(8,128)(2,1)S(1)} %bitcast.34), channel_id=1, source_target_pairs={{0,8},{8,0},{16,24},{24,16},{1,9},{9,1},{17,25},{25,17},{2,10},{10... | collective-permute-start | bytes 1572872 | tf_op jit(solution)/shard_map/ppermute | solution.py:19
  115.4 21.3 %collective-permute-start.17 = (bf16[1,1024,256]{2,1,0:T(8,128)(2,1)S(1)}, bf16[1,1024,256]{2,1,0:T(8,128)(2,1)S(1)}, u32[]{:S(2)}, u32[]{:S(2)}) collective-permute-start(bf16[1,1024,256]{2,1,0:T(8,128)(2,1)S(1)} %collective-permute-done.16.refs_14_), channel_id=1, source_target_pairs={{0,8},{8,0},{16,24},{24,16},{1,9},{9,1},{17,25},{25,17},{2,10},{10... | collective-permute-start | bytes 1572872 | tf_op jit(solution)/shard_map/ppermute | solution.py:19
  115.9 22.3 %collective-permute-start.20 = (bf16[1,1024,256]{2,1,0:T(8,128)(2,1)S(1)}, bf16[1,1024,256]{2,1,0:T(8,128)(2,1)S(1)}, u32[]{:S(2)}, u32[]{:S(2)}) collective-permute-start(bf16[1,1024,256]{2,1,0:T(8,128)(2,1)S(1)} %bitcast.35), channel_id=1, source_target_pairs={{0,16},{8,24},{16,0},{24,8},{1,17},{9,25},{17,1},{25,9},{2,18},{10... | collective-permute-start | bytes 1572872 | tf_op jit(solution)/shard_map/ppermute | solution.py:19
  117.4 20.7 %collective-permute-start.22 = (bf16[384,256]{1,0:T(8,128)(2,1)S(1)}, bf16[384,256]{1,0:T(8,128)(2,1)S(1)}, u32[]{:S(2)}, u32[]{:S(2)}) collective-permute-start(bf16[384,256]{1,0:T(8,128)(2,1)S(1)} %get-tuple-element.87), channel_id=1, source_target_pairs={{0,2},{1,3},{2,0},{3,1},{4,6},{5,7},{6,4},{7,5},{8,10},{9,11},{10,... | collective-permute-start | bytes 589832 | tf_op jit(solution)/shard_map/ppermute | solution.py:19
  119.0 19.2 %collective-permute-start.25 = (bf16[384,256]{1,0:T(8,128)(2,1)S(1)}, bf16[384,256]{1,0:T(8,128)(2,1)S(1)}, u32[]{:S(2)}, u32[]{:S(2)}) collective-permute-start(bf16[384,256]{1,0:T(8,128)(2,1)S(1)} %get-tuple-element.93), channel_id=1, source_target_pairs={{0,4},{1,5},{2,6},{3,7},{4,0},{5,1},{6,2},{7,3},{8,12},{9,13},{10,... | collective-permute-start | bytes 589832 | tf_op jit(solution)/shard_map/ppermute | solution.py:19
  136.6 14.9 %collective-permute-start.21 = (bf16[1,1024,256]{2,1,0:T(8,128)(2,1)S(1)}, bf16[1,1024,256]{2,1,0:T(8,128)(2,1)S(1)}, u32[]{:S(2)}, u32[]{:S(2)}) collective-permute-start(bf16[1,1024,256]{2,1,0:T(8,128)(2,1)S(1)} %collective-permute-done.19.refs_17_), channel_id=1, source_target_pairs={{0,16},{8,24},{16,0},{24,8},{1,17},{9,25},{17,1},{25,9},{2,18},{10... | collective-permute-start | bytes 1572872 | tf_op jit(solution)/shard_map/ppermute | solution.py:19
  138.3 22.7 %collective-permute-start.34 = (bf16[3,384,256]{2,1,0:T(8,128)(2,1)S(1)}, bf16[3,384,256]{2,1,0:T(8,128)(2,1)S(1)}, u32[]{:S(2)}, u32[]{:S(2)}) collective-permute-start(bf16[3,384,256]{2,1,0:T(8,128)(2,1)S(1)} %pad_maximum_fusion.refs_20_), channel_id=1, source_target_pairs={{0,16},{8,24},{16,0},{24,8},{1,17},{9,25},{17,1},{25,9},{2,18},{10... | collective-permute-start | bytes 1769480 | tf_op jit(solution)/shard_map/ppermute | solution.py:19
  138.8 25.3 %collective-permute-start.31 = (bf16[3,384,256]{2,1,0:T(8,128)(2,1)S(1)}, bf16[3,384,256]{2,1,0:T(8,128)(2,1)S(1)}, u32[]{:S(2)}, u32[]{:S(2)}) collective-permute-start(bf16[3,384,256]{2,1,0:T(8,128)(2,1)S(1)} %pad_maximum_fusion.refs_20_), channel_id=1, source_target_pairs={{0,8},{8,0},{16,24},{24,16},{1,9},{9,1},{17,25},{25,17},{2,10},{10... | collective-permute-start | bytes 1769480 | tf_op jit(solution)/shard_map/ppermute | solution.py:19
  140.3 22.1 %collective-permute-start.23 = (bf16[320,256]{1,0:T(8,128)(2,1)S(1)}, bf16[320,256]{1,0:T(8,128)(2,1)S(1)}, u32[]{:S(2)}, u32[]{:S(2)}) collective-permute-start(bf16[320,256]{1,0:T(8,128)(2,1)S(1)} %get-tuple-element.88), channel_id=1, source_target_pairs={{0,2},{1,3},{2,0},{3,1},{4,6},{5,7},{6,4},{7,5},{8,10},{9,11},{10,... | collective-permute-start | bytes 491528 | tf_op jit(solution)/shard_map/ppermute | solution.py:19
  140.3 22.1 %collective-permute-start.26 = (bf16[320,256]{1,0:T(8,128)(2,1)S(1)}, bf16[320,256]{1,0:T(8,128)(2,1)S(1)}, u32[]{:S(2)}, u32[]{:S(2)}) collective-permute-start(bf16[320,256]{1,0:T(8,128)(2,1)S(1)} %get-tuple-element.94), channel_id=1, source_target_pairs={{0,4},{1,5},{2,6},{3,7},{4,0},{5,1},{6,2},{7,3},{8,12},{9,13},{10,... | collective-permute-start | bytes 491528 | tf_op jit(solution)/shard_map/ppermute | solution.py:19
  161.0 22.8 %collective-permute-start.37 = (bf16[3,384,256]{2,1,0:T(8,128)(2,1)S(1)}, bf16[3,384,256]{2,1,0:T(8,128)(2,1)S(1)}, u32[]{:S(2)}, u32[]{:S(2)}) collective-permute-start(bf16[3,384,256]{2,1,0:T(8,128)(2,1)S(1)} %collective-permute-done.34.refs_22_), channel_id=1, source_target_pairs={{0,8},{8,0},{16,24},{24,16},{1,9},{9,1},{17,25},{25,17},{2,10},{10... | collective-permute-start | bytes 1769480 | tf_op jit(solution)/shard_map/ppermute | solution.py:19
  162.5 14.9 %collective-permute-start.35 = (bf16[3,320,256]{2,1,0:T(8,128)(2,1)S(1)}, bf16[3,320,256]{2,1,0:T(8,128)(2,1)S(1)}, u32[]{:S(2)}, u32[]{:S(2)}) collective-permute-start(bf16[3,320,256]{2,1,0:T(8,128)(2,1)S(1)} %pad_maximum_fusion.2.refs_20_), channel_id=1, source_target_pairs={{0,16},{8,24},{16,0},{24,8},{1,17},{9,25},{17,1},{25,9},{2,18},{10... | collective-permute-start | bytes 1474568 | tf_op jit(solution)/shard_map/ppermute | solution.py:19
  164.1 19.6 %collective-permute-start.32 = (bf16[3,320,256]{2,1,0:T(8,128)(2,1)S(1)}, bf16[3,320,256]{2,1,0:T(8,128)(2,1)}, u32[]{:S(2)}, u32[]{:S(2)}) collective-permute-start(bf16[3,320,256]{2,1,0:T(8,128)(2,1)S(1)} %pad_maximum_fusion.2.refs_20_), channel_id=1, source_target_pairs={{0,8},{8,0},{16,24},{24,16},{1,9},{9,1},{17,25},{25,17},{2,10},{10... | collective-permute-start | bytes 1474568 | tf_op jit(solution)/shard_map/ppermute | solution.py:19
  177.5 23.6 %collective-permute-start.36 = (bf16[3,320,256]{2,1,0:T(8,128)(2,1)}, bf16[3,320,256]{2,1,0:T(8,128)(2,1)}, u32[]{:S(2)}, u32[]{:S(2)}) collective-permute-start(bf16[3,320,256]{2,1,0:T(8,128)(2,1)} %pad_maximum_fusion.1.refs_20_), channel_id=1, source_target_pairs={{0,16},{8,24},{16,0},{24,8},{1,17},{9,25},{17,1},{25,9},{2,18},{10... | collective-permute-start | bytes 1474568 | tf_op jit(solution)/shard_map/ppermute | solution.py:19
  184.6 16.5 %collective-permute-start.38 = (bf16[3,320,256]{2,1,0:T(8,128)(2,1)}, bf16[3,320,256]{2,1,0:T(8,128)(2,1)}, u32[]{:S(2)}, u32[]{:S(2)}) collective-permute-start(bf16[3,320,256]{2,1,0:T(8,128)(2,1)} %collective-permute-done.32.refs_21_), channel_id=1, source_target_pairs={{0,16},{8,24},{16,0},{24,8},{1,17},{9,25},{17,1},{25,9},{2,18},{10... | collective-permute-start | bytes 1474568 | tf_op jit(solution)/shard_map/ppermute | solution.py:19
  186.1 27.1 %collective-permute-start.33 = (bf16[3,320,256]{2,1,0:T(8,128)(2,1)}, bf16[3,320,256]{2,1,0:T(8,128)(2,1)S(1)}, u32[]{:S(2)}, u32[]{:S(2)}) collective-permute-start(bf16[3,320,256]{2,1,0:T(8,128)(2,1)} %pad_maximum_fusion.1.refs_20_), channel_id=1, source_target_pairs={{0,8},{8,0},{16,24},{24,16},{1,9},{9,1},{17,25},{25,17},{2,10},{10... | collective-permute-start | bytes 1474568 | tf_op jit(solution)/shard_map/ppermute | solution.py:19
  201.1 12.1 %collective-permute-start.39 = (bf16[3,320,256]{2,1,0:T(8,128)(2,1)}, bf16[3,320,256]{2,1,0:T(8,128)(2,1)S(1)}, u32[]{:S(2)}, u32[]{:S(2)}) collective-permute-start(bf16[3,320,256]{2,1,0:T(8,128)(2,1)} %collective-permute-done.36.refs_22_), channel_id=1, source_target_pairs={{0,8},{8,0},{16,24},{24,16},{1,9},{9,1},{17,25},{25,17},{2,10},{10... | collective-permute-start | bytes 1474568 | tf_op jit(solution)/shard_map/ppermute | solution.py:19
  (35 other events, 1387.4 us)

commit v4 on v3

--- a/solution.py
+++ b/solution.py
@@ -232,11 +232,12 @@
         wait_all(1 - slot)
 
 
-def correlate(frames, first, stop, channels, group, wide, narrow, earlier):
+def correlate(frames, first, stop, channels, group, wide, parted, narrow, earlier):
     groups, count = lax.axis_size("grp"), (wide + narrow)[0][-1].shape[-1]
     block = 2 * PAIRS
     base, steps = first // block, (stop - first) // block
     pieces = [(piece, base) for piece in wide] + [(piece, 0) for piece in narrow]
+    pieces.append((parted[0], (first - parted[1]) // block))
     ordered = [len(piece) == 1 for piece, _ in pieces]
     operands = [array for piece, _ in pieces for array in piece]
     aliases = {} if earlier is None else {1 + len(operands): 0}
@@ -308,18 +309,21 @@
     weights = signs[:, None] * prototype
     at_core = core.reshape(1)
 
-    cuts = [(part * channels, channels) for part in range(parts)]
+    bounds = [round(channels * bound / (32 * PAIRS)) * 2 * PAIRS for bound in BOUNDS]
+    head = bounds[1]
+    cuts = [(0, channels), (channels, head), (channels + head, channels - head)]
+    cuts += [(part * channels, channels) for part in range(2, parts)]
     early = spectra_blocks(False, cuts, at_core, weights, table, [voltages, other])
     own_early = joined(early[0][None], 0)
-    near = swap(early[1], "chan", 2)
+    near, near_rest = swap(early[1], "chan", 2), swap(early[2], "chan", 2)
     near_joined = joined(near[None], 1, own_early)
-    middle = swap(after(early[2], near), "chan", 4)
-    far = [swap(after(early[part], middle), "chan", 2 * part) for part in range(3, parts)]
+    rest_joined = joined(near_rest[None], 1, near_joined)
+    middle = swap(after(early[3], near_rest), "chan", 4)
+    far = [swap(after(early[part + 1], middle), "chan", 2 * part) for part in range(3, parts)]
 
     ahead = lax.optimization_barrier((ahead[0], ahead[1], near, *own_early[1:]))
     halo = jnp.where(core == 0, ahead[0], ahead[1])
-    other_halo = swap(halo, "chan", 1)
-    bounds = [round(channels * bound / (32 * PAIRS)) * 2 * PAIRS for bound in BOUNDS]
+    other_halo = after(swap(halo, "chan", 1), near_rest)
     blocks = list(zip(bounds[:-1], bounds[1:]))
     cuts = [(0, channels)] + [
         (part * channels + first, stop - first)
@@ -327,11 +331,11 @@
         for part in range(1, parts)
     ]
     late = spectra_blocks(True, cuts, at_core, weights, table, [voltages, other, halo, other_halo])
-    own_late = joined(late[0][None], 0, near_joined)
+    own_late = joined(late[0][None], 0, rest_joined)
     middle_joined = joined(middle[None], 1, own_late)
     far_joined = joined(jnp.stack(far), 0, middle_joined)
-    wide = [own_early, near_joined, own_late, middle_joined, far_joined]
-    landed, narrow, results = [near, middle] + far, [far_joined], [None]
+    wide = [own_early, own_late, middle_joined, far_joined]
+    landed, narrow, results = [near_rest, middle] + far, [far_joined], [None]
     for chunk, (first, stop) in enumerate(blocks):
         skipped = chunk * (parts - 1)
         landed = [
@@ -339,10 +343,11 @@
             for part in range(1, parts)
         ]
         events = results[chunk - 1 : chunk] if chunk >= 2 else ()
+        parted = (near_joined, 0) if stop <= head else (rest_joined, head)
         narrow.append(joined(jnp.stack(landed), chunk + 1, narrow[-1], events))
         results.append(
             correlate(
-                frames, first, stop, channels, group.reshape(1), wide, [narrow[-1]], results[-1]
+                frames, first, stop, channels, group.reshape(1), wide, parted, [narrow[-1]], results[-1]
             )
         )
     return results[-1]

time: 229 us -> 232 us (1.013)
  starting transfers between devices: 42.8 us -> 48.7 us
    ppermute x38 -> x42, starting transfers between devices: 37.1 us -> 43 us  [swap(): lax.ppermute(block, axis, [(i, i ^ bit) for i in range(lax.axis_size(axis...]
    unnamed x54 -> x62, local copies, waits for them, and re-layouts: 4.62 us -> 5.38 us
    ppermute x38 -> x42, waiting for transfers between devices: 104 us -> 105 us  [swap(): lax.ppermute(block, axis, [(i, i ^ bit) for i in range(lax.axis_size(axis...]
  transfers between devices with their start and end apart: 40 -> 44, of which waited for: 19 -> 16; matrix products, arithmetic and copies ran while one was open for 3% -> 3% of each run, Pallas kernels for 19% -> 19%
where the time goes in v4:
time: 232 us
  waiting for transfers between devices  114 us (49%)
  Pallas kernels  55.3 us (24%)
  starting transfers between devices  48.7 us (21%)
  local copies, waits for them, and re-layouts  9.7 us (4%)
  other arithmetic  4.15 us (2%)
    ppermute x42, waiting for transfers between devices, swap(): lax.ppermute(block, axis, [(i, i ^ bit) for i in range(lax.axis_size(axis...  105 us
    ppermute x42, starting transfers between devices, swap(): lax.ppermute(block, axis, [(i, i ^ bit) for i in range(lax.axis_size(axis...  43 us
    pallas_call x3, Pallas kernels, correlate(): pl.pallas_call(functools.partial(correlate_kernel, 1.0 / frames, groups,...  36.6 us
    pallas_call x2, Pallas kernels, spectra_blocks(): pl.pallas_call(functools.partial(spectra_kernel, late, cuts, math.sqrt(2....  18.7 us
    ppermute x2, waiting for transfers between devices, on_device(): ahead = [lax.ppermute(sliced[k], 'chan', route[k]) for k in (0, 1)]  8.52 us
    ppermute x2, starting transfers between devices, on_device(): ahead = [lax.ppermute(sliced[k], 'chan', route[k]) for k in (0, 1)]  5.65 us
    unnamed x62, local copies, waits for them, and re-layouts  5.38 us
  transfers between devices with their start and end apart: 44, of which 16 were waited for; matrix products, arithmetic and copies ran while one was open for 3% of the time, Pallas kernels for 19%

profile of v4, /device:TPU:16, one launch (start us, length us, event | category | flops | bytes accessed | tf_op | source)
XLA Modules:
  0.0 231.9 jit_solution(10895606071206094999)
XLA Ops:
  0.0 4.2 %fusion.10 = (bf16[128,7168]{1,0:T(8,128)(2,1)}, bf16[128,7168]{1,0:T(8,128)(2,1)}) fusion(bf16[256,8192]{1,0:T(8,128)(2,1)} %refs_0_.3), kind=kLoop, calls=%fused_computation.33 | loop fusion | bytes 7340032 | tf_op jit(solution)/shard_map/slice | solution.py:302
  4.2 2.3 %collective-permute-start.4 = (bf16[128,7168]{1,0:T(8,128)(2,1)}, bf16[128,7168]{1,0:T(8,128)(2,1)}, u32[]{:S(2)}, u32[]{:S(2)}) collective-permute-start(bf16[128,7168]{1,0:T(8,128)(2,1)} %get-tuple-element.122), channel_id=1, source_target_pairs={{2,0},{4,2},{6,4},{10,8},{12,10},{14,12},{18,16},{20,18},{22,20},{... | collective-permute-start | bytes 5505032 | tf_op jit(solution)/shard_map/ppermute | solution.py:303
  6.6 3.3 %collective-permute-start.5 = (bf16[128,7168]{1,0:T(8,128)(2,1)}, bf16[128,7168]{1,0:T(8,128)(2,1)}, u32[]{:S(2)}, u32[]{:S(2)}) collective-permute-start(bf16[128,7168]{1,0:T(8,128)(2,1)} %get-tuple-element.121), channel_id=1, source_target_pairs={{2,1},{4,3},{6,5},{10,9},{12,11},{14,13},{18,17},{20,19},{22,21},{... | collective-permute-start | bytes 5505032 | tf_op jit(solution)/shard_map/ppermute | solution.py:303
  11.4 2.2 copy-done
  13.6 9.4 %fold_transform.2 = (bf16[1024,256]{1,0:T(8,128)(2,1)S(1)}, bf16[384,256]{1,0:T(8,128)(2,1)S(1)}, bf16[640,256]{1,0:T(8,128)(2,1)S(1)}, bf16[1024,256]{1,0:T(8,128)(2,1)S(1)}, bf16[1024,256]{1,0:T(8,128)(2,1)S(1)}) custom-call(s32[1]{0:T(128)} %bitcast.1.core_ref, f32[8,1024]{1,0:T(8,128)S(1)} %broadcast_multiply_fusion.weights_ref, ...), custom_call_target="tpu_custom_call" | custom-call | flops 1 | bytes 1 | tf_op jit(solution)/shard_map/fold_transform/pallas_call | solution.py:153
  26.1 9.0 %collective-permute-done.1.refs_1_ = bf16[1,1024,256]{2,1,0:T(8,128)(2,1)} collective-permute-done((bf16[1,1024,256]{2,1,0:T(8,128)(2,1)S(1)}, bf16[1,1024,256]{2,1,0:T(8,128)(2,1)}, u32[]{:S(2)}, u32[]{:S(2)}) %collective-permute-start.1) | collective-permute-done | bytes 524320 | tf_op jit(solution)/shard_map/ppermute | solution.py:19
  36.6 2.1 collective-permute-start.6
  38.8 8.5 %collective-permute-done.5 = bf16[128,7168]{1,0:T(8,128)(2,1)} collective-permute-done((bf16[128,7168]{1,0:T(8,128)(2,1)}, bf16[128,7168]{1,0:T(8,128)(2,1)}, u32[]{:S(2)}, u32[]{:S(2)}) %collective-permute-start.5) | collective-permute-done | bytes 1835040 | tf_op jit(solution)/shard_map/ppermute | solution.py:303
  47.3 6.1 %collective-permute-done.6 = bf16[384,256]{1,0:T(8,128)(2,1)S(1)} collective-permute-done((bf16[384,256]{1,0:T(8,128)(2,1)S(1)}, bf16[384,256]{1,0:T(8,128)(2,1)S(1)}, u32[]{:S(2)}, u32[]{:S(2)}) %collective-permute-start.6) | collective-permute-done | bytes 196640 | tf_op jit(solution)/shard_map/ppermute | solution.py:19
  53.4 1.8 broadcast_select_fusion.refs_2_
  58.5 7.0 %collective-permute-done.8 = bf16[640,256]{1,0:T(8,128)(2,1)S(1)} collective-permute-done((bf16[640,256]{1,0:T(8,128)(2,1)S(1)}, bf16[640,256]{1,0:T(8,128)(2,1)S(1)}, u32[]{:S(2)}, u32[]{:S(2)}) %collective-permute-start.8) | collective-permute-done | bytes 327712 | tf_op jit(solution)/shard_map/ppermute | solution.py:19
  69.5 9.3 %fold_transform.3 = (bf16[1024,256]{1,0:T(8,128)(2,1)S(1)}, bf16[384,256]{1,0:T(8,128)(2,1)S(1)}, bf16[384,256]{1,0:T(8,128)(2,1)S(1)}, bf16[384,256]{1,0:T(8,12...) custom-call(s32[1]{0:T(128)} %bitcast.1.core_ref, ...), custom_call_target="tpu_custom_call" | custom-call | flops 1 | bytes 1 | tf_op jit(solution)/shard_map/fold_transform/pallas_call | solution.py:153
  79.7 1.8 collective-permute-start.15
  81.5 14.0 %collective-permute-done.15.refs_23_ = bf16[1,384,256]{2,1,0:T(8,128)(2,1)} collective-permute-done((bf16[1,384,256]{2,1,0:T(8,128)(2,1)S(1)}, bf16[1,384,256]{2,1,0:T(8,128)(2,1)}, u32[]{:S(2)}, u32[]{:S(2)}) %collective-permute-start.15) | collective-permute-done | bytes 196640 | tf_op jit(solution)/shard_map/ppermute | solution.py:19
  96.1 1.6 collective-permute-start.22
  99.7 6.4 %collective-permute-done.16.refs_23_ = bf16[1,640,256]{2,1,0:T(8,128)(2,1)S(1)} collective-permute-done((bf16[1,640,256]{2,1,0:T(8,128)(2,1)S(1)}, bf16[1,640,256]{2,1,0:T(8,128)(2,1)S(1)}, u32[]{:S(2)}, u32[]{:S(2)}) %collective-permute-start.16) | collective-permute-done | bytes 327712 | tf_op jit(solution)/shard_map/ppermute | solution.py:19
  106.7 11.6 %collective-permute-done.22 = bf16[1024,256]{1,0:T(8,128)(2,1)S(1)} collective-permute-done((bf16[1024,256]{1,0:T(8,128)(2,1)S(1)}, bf16[1024,256]{1,0:T(8,128)(2,1)S(1)}, u32[]{:S(2)}, u32[]{:S(2)}) %collective-permute-start.22) | collective-permute-done | bytes 524320 | tf_op jit(solution)/shard_map/ppermute | solution.py:19
  122.0 3.3 %collective-permute-start.26 = (bf16[384,256]{1,0:T(8,128)(2,1)S(1)}, bf16[384,256]{1,0:T(8,128)(2,1)S(1)}, u32[]{:S(2)}, u32[]{:S(2)}) collective-permute-start(bf16[384,256]{1,0:T(8,128)(2,1)S(1)} %get-tuple-element.97), channel_id=1, source_target_pairs={{0,2},{1,3},{2,0},{3,1},{4,6},{5,7},{6,4},{7,5},{8,10},{9,11},{10,... | collective-permute-start | bytes 589832 | tf_op jit(solution)/shard_map/ppermute | solution.py:19
  125.4 7.8 %collective-permute-done.23.refs_13_ = bf16[1,1024,256]{2,1,0:T(8,128)(2,1)S(1)} collective-permute-done((bf16[1,1024,256]{2,1,0:T(8,128)(2,1)S(1)}, bf16[1,1024,256]{2,1,0:T(8,128)(2,1)S(1)}, u32[]{:S(2)}, u32[]{:S(2)}) %collective-permute-start.23) | collective-permute-done | bytes 524320 | tf_op jit(solution)/shard_map/ppermute | solution.py:19
  133.2 1.7 collective-permute-start.32
  134.9 7.4 %collective-permute-done.21.refs_11_ = bf16[1,1024,256]{2,1,0:T(8,128)(2,1)S(1)} collective-permute-done((bf16[1,1024,256]{2,1,0:T(8,128)(2,1)S(1)}, bf16[1,1024,256]{2,1,0:T(8,128)(2,1)S(1)}, u32[]{:S(2)}, u32[]{:S(2)}) %collective-permute-start.21) | collective-permute-done | bytes 524320 | tf_op jit(solution)/shard_map/ppermute | solution.py:19
  146.1 2.4 %collective-permute-start.30 = (bf16[320,256]{1,0:T(8,128)(2,1)S(1)}, bf16[320,256]{1,0:T(8,128)(2,1)S(1)}, u32[]{:S(2)}, u32[]{:S(2)}) collective-permute-start(bf16[320,256]{1,0:T(8,128)(2,1)S(1)} %get-tuple-element.104), channel_id=1, source_target_pairs={{0,4},{1,5},{2,6},{3,7},{4,0},{5,1},{6,2},{7,3},{8,12},{9,13},{10,... | collective-permute-start | bytes 491528 | tf_op jit(solution)/shard_map/ppermute | solution.py:19
  148.6 8.6 %collective-permute-done.25.refs_15_ = bf16[1,1024,256]{2,1,0:T(8,128)(2,1)S(1)} collective-permute-done((bf16[1,1024,256]{2,1,0:T(8,128)(2,1)S(1)}, bf16[1,1024,256]{2,1,0:T(8,128)(2,1)S(1)}, u32[]{:S(2)}, u32[]{:S(2)}) %collective-permute-start.25) | collective-permute-done | bytes 524320 | tf_op jit(solution)/shard_map/ppermute | solution.py:19
  158.2 8.7 %collective-permute-done.38.refs_18_ = bf16[3,384,256]{2,1,0:T(8,128)(2,1)S(1)} collective-permute-done((bf16[3,384,256]{2,1,0:T(8,128)(2,1)S(1)}, bf16[3,384,256]{2,1,0:T(8,128)(2,1)S(1)}, u32[]{:S(2)}, u32[]{:S(2)}) %collective-permute-start.38) | collective-permute-done | bytes 589856 | tf_op jit(solution)/shard_map/ppermute | solution.py:19
  166.9 1.6 collective-permute-start.41
  171.4 4.3 %collective-permute-done.28 = bf16[320,256]{1,0:T(8,128)(2,1)S(1)} collective-permute-done((bf16[320,256]{1,0:T(8,128)(2,1)S(1)}, bf16[320,256]{1,0:T(8,128)(2,1)S(1)}, u32[]{:S(2)}, u32[]{:S(2)}) %collective-permute-start.28) | collective-permute-done | bytes 163872 | tf_op jit(solution)/shard_map/ppermute | solution.py:19
  176.2 2.0 collective-permute-done.31
  178.2 5.4 %collective-permute-done.34 = bf16[320,256]{1,0:T(8,128)(2,1)S(1)} collective-permute-done((bf16[320,256]{1,0:T(8,128)(2,1)S(1)}, bf16[320,256]{1,0:T(8,128)(2,1)S(1)}, u32[]{:S(2)}, u32[]{:S(2)}) %collective-permute-start.34) | collective-permute-done | bytes 163872 | tf_op jit(solution)/shard_map/ppermute | solution.py:19
  184.6 5.3 %collective-permute-done.36.refs_17_ = bf16[3,320,256]{2,1,0:T(8,128)(2,1)} collective-permute-done((bf16[3,320,256]{2,1,0:T(8,128)(2,1)S(1)}, bf16[3,320,256]{2,1,0:T(8,128)(2,1)}, u32[]{:S(2)}, u32[]{:S(2)}) %collective-permute-start.36) | collective-permute-done | bytes 491552 | tf_op jit(solution)/shard_map/ppermute | solution.py:19
  192.9 13.3 %correlate.3.refs_24_ = bf16[128,256,1024]{2,1,0:T(8,128)(2,1)} custom-call(s32[1]{0:T(128)} %bitcast.group_ref, bf16[1,1024,256]{2,1,0:T(8,128)(2,1)} %bitcast.22, bf16[1,1024,256]{2,1,0:T(8,128)(2,1)} %collective-permute-done.1.refs_1_, bf16[1,1024,256]{2,1,0:T(8,128)(2,1)} %collective-permute-done.2.refs_2_, ...), custom_call_target="tpu_custom_call" | custom-call | flops 1 | bytes 1 | tf_op jit(solution)/shard_map/correlate/pallas_call | solution.py:253
  206.9 11.6 %correlate.4.refs_24_ = bf16[128,256,1024]{2,1,0:T(8,128)(2,1)} custom-call(s32[1]{0:T(128)} %bitcast.group_ref, bf16[1,1024,256]{2,1,0:T(8,128)(2,1)} %bitcast.23, bf16[1,1024,256]{2,1,0:T(8,128)(2,1)} %collective-permute-done.1.refs_1_, bf16[1,1024,256]{2,1,0:T(8,128)(2,1)} %collective-permute-done.2.refs_2_, ...), custom_call_target="tpu_custom_call", output_to_operand_aliasing={{}: (25, {})} | custom-call | flops 1 | bytes 1 | tf_op jit(solution)/shard_map/correlate/pallas_call | solution.py:253
  220.0 11.7 %correlate.5 = bf16[128,256,1024]{2,1,0:T(8,128)(2,1)} custom-call(s32[1]{0:T(128)} %bitcast.group_ref, bf16[1,1024,256]{2,1,0:T(8,128)(2,1)} %bitcast.24, bf16[1,1024,256]{2,1,0:T(8,128)(2,1)} %collective-permute-done.1.refs_1_, bf16[1,1024,256]{2,1,0:T(8,128)(2,1)} %collective-permute-done.2.refs_2_, ...), custom_call_target="tpu_custom_call", output_to_operand_aliasing={{}: (25, {})} | custom-call | flops 1 | bytes 1 | tf_op jit(solution)/shard_map/correlate/pallas_call | solution.py:253
  (138 shorter events, 35.3 us)
Async XLA Ops:
  4.2 34.5 %collective-permute-start.4 = (bf16[128,7168]{1,0:T(8,128)(2,1)}, bf16[128,7168]{1,0:T(8,128)(2,1)}, u32[]{:S(2)}, u32[]{:S(2)}) collective-permute-start(bf16[128,7168]{1,0:T(8,128)(2,1)} %get-tuple-element.122), channel_id=1, source_target_pairs={{2,0},{4,2},{6,4},{10,8},{12,10},{14,12},{18,16},{20,18},{22,20},{... | collective-permute-start | bytes 5505032 | tf_op jit(solution)/shard_map/ppermute | solution.py:303
  6.6 40.7 %collective-permute-start.5 = (bf16[128,7168]{1,0:T(8,128)(2,1)}, bf16[128,7168]{1,0:T(8,128)(2,1)}, u32[]{:S(2)}, u32[]{:S(2)}) collective-permute-start(bf16[128,7168]{1,0:T(8,128)(2,1)} %get-tuple-element.121), channel_id=1, source_target_pairs={{2,1},{4,3},{6,5},{10,9},{12,11},{14,13},{18,17},{20,19},{22,21},{... | collective-permute-start | bytes 5505032 | tf_op jit(solution)/shard_map/ppermute | solution.py:303
  24.6 28.9 %collective-permute-start.2 = (bf16[1,1024,256]{2,1,0:T(8,128)(2,1)S(1)}, bf16[1,1024,256]{2,1,0:T(8,128)(2,1)}, u32[]{:S(2)}, u32[]{:S(2)}) collective-permute-start(bf16[1,1024,256]{2,1,0:T(8,128)(2,1)S(1)} %bitcast.21), channel_id=1, source_target_pairs={{0,16},{8,24},{16,0},{24,8},{1,17},{9,25},{17,1},{25,9},{2,18},{10... | collective-permute-start | bytes 1572872 | tf_op jit(solution)/shard_map/ppermute | solution.py:19
  35.1 18.3 %collective-permute-start.3 = (bf16[1,1024,256]{2,1,0:T(8,128)(2,1)}, bf16[1,1024,256]{2,1,0:T(8,128)(2,1)}, u32[]{:S(2)}, u32[]{:S(2)}) collective-permute-start(bf16[1,1024,256]{2,1,0:T(8,128)(2,1)} %collective-permute-done.1.refs_1_), channel_id=1, source_target_pairs={{0,16},{8,24},{16,0},{24,8},{1,17},{9,25},{17,1},{25,9},{2,18},{10... | collective-permute-start | bytes 1572872 | tf_op jit(solution)/shard_map/ppermute | solution.py:19
  36.6 16.8 %collective-permute-start.6 = (bf16[384,256]{1,0:T(8,128)(2,1)S(1)}, bf16[384,256]{1,0:T(8,128)(2,1)S(1)}, u32[]{:S(2)}, u32[]{:S(2)}) collective-permute-start(bf16[384,256]{1,0:T(8,128)(2,1)S(1)} %get-tuple-element.69), channel_id=1, source_target_pairs={{0,2},{1,3},{2,0},{3,1},{4,6},{5,7},{6,4},{7,5},{8,10},{9,11},{10,... | collective-permute-start | bytes 589832 | tf_op jit(solution)/shard_map/ppermute | solution.py:19
  55.2 14.3 %collective-permute-start.7 = (bf16[128,7168]{1,0:T(8,128)(2,1)S(1)}, bf16[128,7168]{1,0:T(8,128)(2,1)S(1)}, u32[]{:S(2)}, u32[]{:S(2)}) collective-permute-start(bf16[128,7168]{1,0:T(8,128)(2,1)S(1)} %broadcast_select_fusion.refs_2_), channel_id=1, source_target_pairs={{0,1},{1,0},{2,3},{3,2},{4,5},{5,4},{6,7},{7,6},{8,9},{9,8},{10,11... | collective-permute-start | bytes 5505032 | tf_op jit(solution)/shard_map/ppermute | solution.py:19
  66.2 12.7 %collective-permute-start.10 = (bf16[1,640,256]{2,1,0:T(8,128)(2,1)S(1)}, bf16[1,640,256]{2,1,0:T(8,128)(2,1)S(1)}, u32[]{:S(2)}, u32[]{:S(2)}) collective-permute-start(bf16[1,640,256]{2,1,0:T(8,128)(2,1)S(1)} %bitcast.40), channel_id=1, source_target_pairs={{0,8},{8,0},{16,24},{24,16},{1,9},{9,1},{17,25},{25,17},{2,10},{10... | collective-permute-start | bytes 983048 | tf_op jit(solution)/shard_map/ppermute | solution.py:19
  69.2 26.9 %collective-permute-start.18 = (bf16[1024,256]{1,0:T(8,128)(2,1)S(1)}, bf16[1024,256]{1,0:T(8,128)(2,1)S(1)}, u32[]{:S(2)}, u32[]{:S(2)}) collective-permute-start(bf16[1024,256]{1,0:T(8,128)(2,1)S(1)} %get-tuple-element.85), channel_id=1, source_target_pairs={{0,4},{1,5},{2,6},{3,7},{4,0},{5,1},{6,2},{7,3},{8,12},{9,13},{10,... | collective-permute-start | bytes 1572872 | tf_op jit(solution)/shard_map/ppermute | solution.py:19
  78.9 18.7 %collective-permute-start.11 = (bf16[1,1024,256]{2,1,0:T(8,128)(2,1)S(1)}, bf16[1,1024,256]{2,1,0:T(8,128)(2,1)S(1)}, u32[]{:S(2)}, u32[]{:S(2)}) collective-permute-start(bf16[1,1024,256]{2,1,0:T(8,128)(2,1)S(1)} %bitcast.25), channel_id=1, source_target_pairs={{0,8},{8,0},{16,24},{24,16},{1,9},{9,1},{17,25},{25,17},{2,10},{10... | collective-permute-start | bytes 1572872 | tf_op jit(solution)/shard_map/ppermute | solution.py:19
  79.5 19.7 %collective-permute-start.14 = (bf16[1,1024,256]{2,1,0:T(8,128)(2,1)S(1)}, bf16[1,1024,256]{2,1,0:T(8,128)(2,1)S(1)}, u32[]{:S(2)}, u32[]{:S(2)}) collective-permute-start(bf16[1,1024,256]{2,1,0:T(8,128)(2,1)S(1)} %bitcast.26), channel_id=1, source_target_pairs={{0,16},{8,24},{16,0},{24,8},{1,17},{9,25},{17,1},{25,9},{2,18},{10... | collective-permute-start | bytes 1572872 | tf_op jit(solution)/shard_map/ppermute | solution.py:19
  79.7 15.8 %collective-permute-start.15 = (bf16[1,384,256]{2,1,0:T(8,128)(2,1)S(1)}, bf16[1,384,256]{2,1,0:T(8,128)(2,1)}, u32[]{:S(2)}, u32[]{:S(2)}) collective-permute-start(bf16[1,384,256]{2,1,0:T(8,128)(2,1)S(1)} %collective-permute-done.12.refs_22_), channel_id=1, source_target_pairs={{0,8},{8,0},{16,24},{24,16},{1,9},{9,1},{17,25},{25,17},{2,10},{10... | collective-permute-start | bytes 589832 | tf_op jit(solution)/shard_map/ppermute | solution.py:19
  96.1 22.2 %collective-permute-start.22 = (bf16[1024,256]{1,0:T(8,128)(2,1)S(1)}, bf16[1024,256]{1,0:T(8,128)(2,1)S(1)}, u32[]{:S(2)}, u32[]{:S(2)}) collective-permute-start(bf16[1024,256]{1,0:T(8,128)(2,1)S(1)} %get-tuple-element.90), channel_id=1, source_target_pairs={{0,6},{1,7},{2,4},{3,5},{4,2},{5,3},{6,0},{7,1},{8,14},{9,15},{10,... | collective-permute-start | bytes 1572872 | tf_op jit(solution)/shard_map/ppermute | solution.py:19
  97.7 20.6 %collective-permute-start.19 = (bf16[1,1024,256]{2,1,0:T(8,128)(2,1)S(1)}, bf16[1,1024,256]{2,1,0:T(8,128)(2,1)S(1)}, u32[]{:S(2)}, u32[]{:S(2)}) collective-permute-start(bf16[1,1024,256]{2,1,0:T(8,128)(2,1)S(1)} %bitcast.30), channel_id=1, source_target_pairs={{0,8},{8,0},{16,24},{24,16},{1,9},{9,1},{17,25},{25,17},{2,10},{10... | collective-permute-start | bytes 1572872 | tf_op jit(solution)/shard_map/ppermute | solution.py:19
  99.2 20.6 %collective-permute-start.20 = (bf16[1,1024,256]{2,1,0:T(8,128)(2,1)S(1)}, bf16[1,1024,256]{2,1,0:T(8,128)(2,1)S(1)}, u32[]{:S(2)}, u32[]{:S(2)}) collective-permute-start(bf16[1,1024,256]{2,1,0:T(8,128)(2,1)S(1)} %bitcast.31), channel_id=1, source_target_pairs={{0,16},{8,24},{16,0},{24,8},{1,17},{9,25},{17,1},{25,9},{2,18},{10... | collective-permute-start | bytes 1572872 | tf_op jit(solution)/shard_map/ppermute | solution.py:19
  106.2 14.8 %collective-permute-start.17 = (bf16[1,1024,256]{2,1,0:T(8,128)(2,1)S(1)}, bf16[1,1024,256]{2,1,0:T(8,128)(2,1)S(1)}, u32[]{:S(2)}, u32[]{:S(2)}) collective-permute-start(bf16[1,1024,256]{2,1,0:T(8,128)(2,1)S(1)} %collective-permute-done.11.refs_5_), channel_id=1, source_target_pairs={{0,16},{8,24},{16,0},{24,8},{1,17},{9,25},{17,1},{25,9},{2,18},{10... | collective-permute-start | bytes 1572872 | tf_op jit(solution)/shard_map/ppermute | solution.py:19
  118.2 14.9 %collective-permute-start.23 = (bf16[1,1024,256]{2,1,0:T(8,128)(2,1)S(1)}, bf16[1,1024,256]{2,1,0:T(8,128)(2,1)S(1)}, u32[]{:S(2)}, u32[]{:S(2)}) collective-permute-start(bf16[1,1024,256]{2,1,0:T(8,128)(2,1)S(1)} %bitcast.35), channel_id=1, source_target_pairs={{0,8},{8,0},{16,24},{24,16},{1,9},{9,1},{17,25},{25,17},{2,10},{10... | collective-permute-start | bytes 1572872 | tf_op jit(solution)/shard_map/ppermute | solution.py:19
  121.0 21.3 %collective-permute-start.21 = (bf16[1,1024,256]{2,1,0:T(8,128)(2,1)S(1)}, bf16[1,1024,256]{2,1,0:T(8,128)(2,1)S(1)}, u32[]{:S(2)}, u32[]{:S(2)}) collective-permute-start(bf16[1,1024,256]{2,1,0:T(8,128)(2,1)S(1)} %collective-permute-done.20.refs_10_), channel_id=1, source_target_pairs={{0,8},{8,0},{16,24},{24,16},{1,9},{9,1},{17,25},{25,17},{2,10},{10... | collective-permute-start | bytes 1572872 | tf_op jit(solution)/shard_map/ppermute | solution.py:19
  121.5 21.7 %collective-permute-start.24 = (bf16[1,1024,256]{2,1,0:T(8,128)(2,1)S(1)}, bf16[1,1024,256]{2,1,0:T(8,128)(2,1)S(1)}, u32[]{:S(2)}, u32[]{:S(2)}) collective-permute-start(bf16[1,1024,256]{2,1,0:T(8,128)(2,1)S(1)} %bitcast.36), channel_id=1, source_target_pairs={{0,16},{8,24},{16,0},{24,8},{1,17},{9,25},{17,1},{25,9},{2,18},{10... | collective-permute-start | bytes 1572872 | tf_op jit(solution)/shard_map/ppermute | solution.py:19
  122.0 21.0 %collective-permute-start.26 = (bf16[384,256]{1,0:T(8,128)(2,1)S(1)}, bf16[384,256]{1,0:T(8,128)(2,1)S(1)}, u32[]{:S(2)}, u32[]{:S(2)}) collective-permute-start(bf16[384,256]{1,0:T(8,128)(2,1)S(1)} %get-tuple-element.97), channel_id=1, source_target_pairs={{0,2},{1,3},{2,0},{3,1},{4,6},{5,7},{6,4},{7,5},{8,10},{9,11},{10,... | collective-permute-start | bytes 589832 | tf_op jit(solution)/shard_map/ppermute | solution.py:19
  125.4 17.7 %collective-permute-start.29 = (bf16[384,256]{1,0:T(8,128)(2,1)S(1)}, bf16[384,256]{1,0:T(8,128)(2,1)S(1)}, u32[]{:S(2)}, u32[]{:S(2)}) collective-permute-start(bf16[384,256]{1,0:T(8,128)(2,1)S(1)} %get-tuple-element.103), channel_id=1, source_target_pairs={{0,4},{1,5},{2,6},{3,7},{4,0},{5,1},{6,2},{7,3},{8,12},{9,13},{10,... | collective-permute-start | bytes 589832 | tf_op jit(solution)/shard_map/ppermute | solution.py:19
  142.4 14.9 %collective-permute-start.25 = (bf16[1,1024,256]{2,1,0:T(8,128)(2,1)S(1)}, bf16[1,1024,256]{2,1,0:T(8,128)(2,1)S(1)}, u32[]{:S(2)}, u32[]{:S(2)}) collective-permute-start(bf16[1,1024,256]{2,1,0:T(8,128)(2,1)S(1)} %collective-permute-done.23.refs_13_), channel_id=1, source_target_pairs={{0,16},{8,24},{16,0},{24,8},{1,17},{9,25},{17,1},{25,9},{2,18},{10... | collective-permute-start | bytes 1572872 | tf_op jit(solution)/shard_map/ppermute | solution.py:19
  143.2 23.7 %collective-permute-start.38 = (bf16[3,384,256]{2,1,0:T(8,128)(2,1)S(1)}, bf16[3,384,256]{2,1,0:T(8,128)(2,1)S(1)}, u32[]{:S(2)}, u32[]{:S(2)}) collective-permute-start(bf16[3,384,256]{2,1,0:T(8,128)(2,1)S(1)} %pad_maximum_fusion.refs_16_), channel_id=1, source_target_pairs={{0,16},{8,24},{16,0},{24,8},{1,17},{9,25},{17,1},{25,9},{2,18},{10... | collective-permute-start | bytes 1769480 | tf_op jit(solution)/shard_map/ppermute | solution.py:19
  144.6 24.6 %collective-permute-start.35 = (bf16[3,384,256]{2,1,0:T(8,128)(2,1)S(1)}, bf16[3,384,256]{2,1,0:T(8,128)(2,1)S(1)}, u32[]{:S(2)}, u32[]{:S(2)}) collective-permute-start(bf16[3,384,256]{2,1,0:T(8,128)(2,1)S(1)} %pad_maximum_fusion.refs_16_), channel_id=1, source_target_pairs={{0,8},{8,0},{16,24},{24,16},{1,9},{9,1},{17,25},{25,17},{2,10},{10... | collective-permute-start | bytes 1769480 | tf_op jit(solution)/shard_map/ppermute | solution.py:19
  146.1 22.4 %collective-permute-start.27 = (bf16[320,256]{1,0:T(8,128)(2,1)S(1)}, bf16[320,256]{1,0:T(8,128)(2,1)S(1)}, u32[]{:S(2)}, u32[]{:S(2)}) collective-permute-start(bf16[320,256]{1,0:T(8,128)(2,1)S(1)} %get-tuple-element.98), channel_id=1, source_target_pairs={{0,2},{1,3},{2,0},{3,1},{4,6},{5,7},{6,4},{7,5},{8,10},{9,11},{10,... | collective-permute-start | bytes 491528 | tf_op jit(solution)/shard_map/ppermute | solution.py:19
  146.1 22.4 %collective-permute-start.30 = (bf16[320,256]{1,0:T(8,128)(2,1)S(1)}, bf16[320,256]{1,0:T(8,128)(2,1)S(1)}, u32[]{:S(2)}, u32[]{:S(2)}) collective-permute-start(bf16[320,256]{1,0:T(8,128)(2,1)S(1)} %get-tuple-element.104), channel_id=1, source_target_pairs={{0,4},{1,5},{2,6},{3,7},{4,0},{5,1},{6,2},{7,3},{8,12},{9,13},{10,... | collective-permute-start | bytes 491528 | tf_op jit(solution)/shard_map/ppermute | solution.py:19
  166.9 23.0 %collective-permute-start.41 = (bf16[3,384,256]{2,1,0:T(8,128)(2,1)S(1)}, bf16[3,384,256]{2,1,0:T(8,128)(2,1)S(1)}, u32[]{:S(2)}, u32[]{:S(2)}) collective-permute-start(bf16[3,384,256]{2,1,0:T(8,128)(2,1)S(1)} %collective-permute-done.38.refs_18_), channel_id=1, source_target_pairs={{0,8},{8,0},{16,24},{24,16},{1,9},{9,1},{17,25},{25,17},{2,10},{10... | collective-permute-start | bytes 1769480 | tf_op jit(solution)/shard_map/ppermute | solution.py:19
  168.6 16.0 %collective-permute-start.39 = (bf16[3,320,256]{2,1,0:T(8,128)(2,1)S(1)}, bf16[3,320,256]{2,1,0:T(8,128)(2,1)S(1)}, u32[]{:S(2)}, u32[]{:S(2)}) collective-permute-start(bf16[3,320,256]{2,1,0:T(8,128)(2,1)S(1)} %pad_maximum_fusion.2.refs_16_), channel_id=1, source_target_pairs={{0,16},{8,24},{16,0},{24,8},{1,17},{9,25},{17,1},{25,9},{2,18},{10... | collective-permute-start | bytes 1474568 | tf_op jit(solution)/shard_map/ppermute | solution.py:19
  169.2 20.7 %collective-permute-start.36 = (bf16[3,320,256]{2,1,0:T(8,128)(2,1)S(1)}, bf16[3,320,256]{2,1,0:T(8,128)(2,1)}, u32[]{:S(2)}, u32[]{:S(2)}) collective-permute-start(bf16[3,320,256]{2,1,0:T(8,128)(2,1)S(1)} %pad_maximum_fusion.2.refs_16_), channel_id=1, source_target_pairs={{0,8},{8,0},{16,24},{24,16},{1,9},{9,1},{17,25},{25,17},{2,10},{10... | collective-permute-start | bytes 1474568 | tf_op jit(solution)/shard_map/ppermute | solution.py:19
  184.5 21.7 %collective-permute-start.40 = (bf16[3,320,256]{2,1,0:T(8,128)(2,1)}, bf16[3,320,256]{2,1,0:T(8,128)(2,1)}, u32[]{:S(2)}, u32[]{:S(2)}) collective-permute-start(bf16[3,320,256]{2,1,0:T(8,128)(2,1)} %pad_maximum_fusion.1.refs_16_), channel_id=1, source_target_pairs={{0,16},{8,24},{16,0},{24,8},{1,17},{9,25},{17,1},{25,9},{2,18},{10... | collective-permute-start | bytes 1474568 | tf_op jit(solution)/shard_map/ppermute | solution.py:19
  190.7 15.5 %collective-permute-start.42 = (bf16[3,320,256]{2,1,0:T(8,128)(2,1)}, bf16[3,320,256]{2,1,0:T(8,128)(2,1)}, u32[]{:S(2)}, u32[]{:S(2)}) collective-permute-start(bf16[3,320,256]{2,1,0:T(8,128)(2,1)} %collective-permute-done.36.refs_17_), channel_id=1, source_target_pairs={{0,16},{8,24},{16,0},{24,8},{1,17},{9,25},{17,1},{25,9},{2,18},{10... | collective-permute-start | bytes 1474568 | tf_op jit(solution)/shard_map/ppermute | solution.py:19
  191.5 27.0 %collective-permute-start.37 = (bf16[3,320,256]{2,1,0:T(8,128)(2,1)}, bf16[3,320,256]{2,1,0:T(8,128)(2,1)S(1)}, u32[]{:S(2)}, u32[]{:S(2)}) collective-permute-start(bf16[3,320,256]{2,1,0:T(8,128)(2,1)} %pad_maximum_fusion.1.refs_16_), channel_id=1, source_target_pairs={{0,8},{8,0},{16,24},{24,16},{1,9},{9,1},{17,25},{25,17},{2,10},{10... | collective-permute-start | bytes 1474568 | tf_op jit(solution)/shard_map/ppermute | solution.py:19
  206.3 12.2 %collective-permute-start.43 = (bf16[3,320,256]{2,1,0:T(8,128)(2,1)}, bf16[3,320,256]{2,1,0:T(8,128)(2,1)S(1)}, u32[]{:S(2)}, u32[]{:S(2)}) collective-permute-start(bf16[3,320,256]{2,1,0:T(8,128)(2,1)} %collective-permute-done.40.refs_18_), channel_id=1, source_target_pairs={{0,8},{8,0},{16,24},{24,16},{1,9},{9,1},{17,25},{25,17},{2,10},{10... | collective-permute-start | bytes 1474568 | tf_op jit(solution)/shard_map/ppermute | solution.py:19
  (43 other events, 1405.7 us)
